TPU v7x, 32 devices: a whole 2x2x4 slice. The times are simulated.
32 devices in a mesh: dp: 8 (over z, y), expert: 4 (over x, core).
Axes of the slice: x: 2, y: 2, z: 4, core: 2. Of those that a mesh axis runs over, the one named last changes fastest.
Arguments:
- inputs: bfloat16 [4, 96, 197, 768], P(None, ('dp', 'expert')), may hold values from -6 to 6
- counts: int32 [4, 32], P(None, ('dp', 'expert')), may hold values from 1 to 3, 64 in all within a row
- ln1_gain: bfloat16 [768], P(('dp', 'expert')), may hold values from 0.099609375 to 1.8984375
- ln1_bias: bfloat16 [768], P(('dp', 'expert')), may hold values from -1.5 to 1.5
- w_qkv: bfloat16 [768, 2304], P(('dp', 'expert')), may hold values from -0.21875 to 0.21875
- w_out: bfloat16 [768, 768], P(('dp', 'expert')), may hold values from -0.625 to 0.625
- ln2_gain: bfloat16 [768], P(('dp', 'expert')), may hold values from 0.099609375 to 1.8984375
- ln2_bias: bfloat16 [768], P(('dp', 'expert')), may hold values from -1.5 to 1.5
- phi: bfloat16 [768, 8], P(('dp', 'expert')), may hold values from -0.125 to 0.125
- w_up: bfloat16 [8, 768, 3072], P('expert', None, 'dp'), may hold values from -1.75 to 1.75
- w_down: bfloat16 [8, 3072, 768], P('expert', 'dp'), may hold values from -0.4375 to 0.4375
- cotangent: bfloat16 [4, 96, 197, 768], P(None, ('dp', 'expert')), may hold values from -6 to 6
Outputs:
- output: bfloat16 [4, 96, 197, 768], P(None, ('dp', 'expert'))
- input_grad: bfloat16 [4, 96, 197, 768], P(None, ('dp', 'expert'))
- grad_ln1_gain: float32 [768], P(('dp', 'expert'))
- grad_ln1_bias: float32 [768], P(('dp', 'expert'))
- grad_w_qkv: float32 [768, 2304], P(('dp', 'expert'))
- grad_w_out: float32 [768, 768], P(('dp', 'expert'))
- grad_ln2_gain: float32 [768], P(('dp', 'expert'))
- grad_ln2_bias: float32 [768], P(('dp', 'expert'))
- grad_phi: float32 [768, 8], P(('dp', 'expert'))
- grad_w_up: float32 [8, 768, 3072], P('expert', None, 'dp')
- grad_w_down: float32 [8, 3072, 768], P('expert', 'dp')
Inputs may be any that keep to these rules, and one draw needn't show every extreme that they name: counts[b, d] is how many of device d's first 3 image places hold live images in micro-batch b; each micro-batch holds 64 live images and some device is full.
All inputs are finite; a program needn't handle non-finite values.
Results may differ from a plain program's by a relative error of at most 0.018.
Values may be sent and summed in bfloat16 or wider, within the bound.
No kernel may reach another device: no remote copies, remote signals or barrier semaphores. Data moves between devices by JAX's collectives and lax.ppermute only.
A program may use at most 384 MiB of HBM per device.

v0:
```python
from functools import partial

import jax
import jax.numpy as jnp
from jax import lax
from jax.sharding import PartitionSpec as P

HEADS = 12
HEAD_DIM = 64


EPSILON = 1e-06


def round_down(v):
    return lax.optimization_barrier(v.astype(jnp.bfloat16)).astype(jnp.float32)


def same_value(v):
    return v


def make_rounders():
    rounded = jax.custom_vjp(round_down)
    rounded.defvjp(lambda v: (round_down(v), None), lambda kept, grad: (grad,))
    back_rounded = jax.custom_vjp(same_value)
    back_rounded.defvjp(lambda v: (v, None), lambda kept, grad: (round_down(grad),))
    return (rounded, back_rounded)


def normalize(values, norm_gain, norm_bias):
    center = values - jnp.mean(values, axis=-1, keepdims=True)
    spread = jnp.mean(center * center, axis=-1, keepdims=True)
    return center * lax.rsqrt(spread + EPSILON) * norm_gain + norm_bias


def softmax_along(values, dimension):
    largest = jnp.max(values, axis=dimension, keepdims=True)
    powers = jnp.exp(values - largest)
    return powers / jnp.sum(powers, axis=dimension, keepdims=True)


def mixer_part(inputs, ln1_gain, ln1_bias, w_qkv, w_out, ln2_gain, ln2_bias, phi):
    rounded, back_rounded = make_rounders()
    images, length, features = inputs.shape
    normed = rounded(normalize(inputs, ln1_gain, ln1_bias))
    triple = back_rounded(rounded(jnp.einsum("gtd,de->gte", normed, w_qkv)))
    triple = triple.reshape(images, length, 3, HEADS, HEAD_DIM)
    queries = triple[:, :, 0]
    keys_all = triple[:, :, 1]
    values_all = triple[:, :, 2]
    scores = back_rounded(jnp.einsum("gqhc,gkhc->ghqk", queries, keys_all) * HEAD_DIM ** (-0.5))
    attention = rounded(softmax_along(scores, 3))
    mixed_heads = jnp.einsum("ghqk,gkhc->gqhc", attention, values_all)
    mixed_heads = back_rounded(rounded(mixed_heads.reshape(images, length, features)))
    branch = back_rounded(jnp.einsum("gtd,de->gte", mixed_heads, w_out))
    hidden_state = inputs + branch
    normed_two = rounded(normalize(hidden_state, ln2_gain, ln2_bias))
    logits = back_rounded(jnp.einsum("gtd,ds->gts", normed_two, phi))
    dispatch = rounded(softmax_along(logits, 1))
    combine = rounded(softmax_along(logits, 2))
    slot_in = back_rounded(rounded(jnp.einsum("gts,gtd->gsd", dispatch, normed_two)))
    return (hidden_state, combine, slot_in)


def combine_part(hidden_state, combine, slot_out):
    rounded, back_rounded = make_rounders()
    slot_out = back_rounded(slot_out)
    return hidden_state + jnp.einsum("gts,gsd->gtd", combine, slot_out)


def expert_forward(slot_rows, up_weight, down_weight):
    pre_act = jnp.einsum("rsd,sdf->rsf", slot_rows, up_weight, preferred_element_type=jnp.float32)
    active = jax.nn.gelu(pre_act, approximate=False).astype(jnp.bfloat16)
    produced = jnp.einsum("rsf,sfd->rsd", active, down_weight, preferred_element_type=jnp.float32)
    return (pre_act, active, produced)


def expert_backward(slot_rows, up_weight, down_weight, pre_act, active, grad_out):
    grad_active = jnp.einsum(
        "rsd,sfd->rsf", grad_out, down_weight, preferred_element_type=jnp.float32
    )
    unused, slope_back = jax.vjp(partial(jax.nn.gelu, approximate=False), pre_act)
    grad_pre = slope_back(grad_active)[0].astype(jnp.bfloat16)
    grad_down = jnp.einsum("rsf,rsd->sfd", active, grad_out, preferred_element_type=jnp.float32)
    grad_up = jnp.einsum("rsd,rsf->sdf", slot_rows, grad_pre, preferred_element_type=jnp.float32)
    grad_rows = jnp.einsum("rsf,sdf->rsd", grad_pre, up_weight, preferred_element_type=jnp.float32)
    return (grad_rows, grad_up, grad_down)


def body(
    inputs,
    counts,
    ln1_gain,
    ln1_bias,
    w_qkv,
    w_out,
    ln2_gain,
    ln2_bias,
    phi,
    w_up,
    w_down,
    cotangent,
):
    batches = inputs.shape[0]
    capacity = inputs.shape[1]
    outputs = []
    grads_in = []
    dense_sums = None
    expert_sums = None
    for micro_index in range(batches):
        gathered = (
            lax.all_gather(ln1_gain, ("dp", "expert"), axis=0, tiled=True),
            lax.all_gather(ln1_bias, ("dp", "expert"), axis=0, tiled=True),
            lax.all_gather(w_qkv, ("dp", "expert"), axis=0, tiled=True),
            lax.all_gather(w_out, ("dp", "expert"), axis=0, tiled=True),
            lax.all_gather(ln2_gain, ("dp", "expert"), axis=0, tiled=True),
            lax.all_gather(ln2_bias, ("dp", "expert"), axis=0, tiled=True),
            lax.all_gather(phi, ("dp", "expert"), axis=0, tiled=True),
        )
        dense_now = tuple((member.astype(jnp.float32) for member in gathered))
        expert_now = (
            lax.all_gather(w_up, "dp", axis=2, tiled=True),
            lax.all_gather(w_down, "dp", axis=1, tiled=True),
        )
        live_mask = (jnp.arange(capacity) < counts[micro_index, 0]).astype(jnp.float32)[
            :, None, None
        ]
        image_in = inputs[micro_index].astype(jnp.float32)
        (hidden_state, combine, slot_in), mixer_back = jax.vjp(mixer_part, image_in, *dense_now)
        arrived = lax.all_to_all(
            slot_in.astype(jnp.bfloat16), "expert", split_axis=1, concat_axis=0, tiled=True
        )
        pre_act, active, produced = expert_forward(arrived, expert_now[0], expert_now[1])
        returned = lax.all_to_all(
            produced.astype(jnp.bfloat16), "expert", split_axis=0, concat_axis=1, tiled=True
        )
        result, combine_back = jax.vjp(
            combine_part, hidden_state, combine, returned.astype(jnp.float32)
        )
        outputs.append((result * live_mask).astype(jnp.bfloat16))
        grad_result = cotangent[micro_index].astype(jnp.float32) * live_mask
        grad_hidden, grad_combine, grad_slot = combine_back(grad_result)
        grad_arrived = lax.all_to_all(
            grad_slot.astype(jnp.bfloat16), "expert", split_axis=1, concat_axis=0, tiled=True
        )
        grad_rows, grad_up, grad_down = expert_backward(
            arrived, expert_now[0], expert_now[1], pre_act, active, grad_arrived
        )
        grad_slot_in = lax.all_to_all(
            grad_rows.astype(jnp.bfloat16), "expert", split_axis=0, concat_axis=1, tiled=True
        )
        mixer_grads = mixer_back((grad_hidden, grad_combine, grad_slot_in.astype(jnp.float32)))
        grads_in.append(mixer_grads[0].astype(jnp.bfloat16))
        if dense_sums is None:
            dense_sums = tuple(mixer_grads[1:])
            expert_sums = (grad_up, grad_down)
        else:
            dense_sums = tuple((older + newer for older, newer in zip(dense_sums, mixer_grads[1:])))
            expert_sums = (expert_sums[0] + grad_up, expert_sums[1] + grad_down)
    dense_out = lax.psum_scatter(dense_sums, ("dp", "expert"), scatter_dimension=0, tiled=True)
    expert_out = (
        lax.psum_scatter(
            expert_sums[0].astype(jnp.bfloat16), "dp", scatter_dimension=2, tiled=True
        ).astype(jnp.float32),
        lax.psum_scatter(
            expert_sums[1].astype(jnp.bfloat16), "dp", scatter_dimension=1, tiled=True
        ).astype(jnp.float32),
    )
    return (
        jnp.stack(outputs),
        jnp.stack(grads_in),
        dense_out[0],
        dense_out[1],
        dense_out[2],
        dense_out[3],
        dense_out[4],
        dense_out[5],
        dense_out[6],
        expert_out[0],
        expert_out[1],
    )


def solution(mesh):
    placed = (
        P(None, ("dp", "expert"), None, None),
        P(None, ("dp", "expert")),
        P(("dp", "expert")),
        P(("dp", "expert")),
        P(("dp", "expert"), None),
        P(("dp", "expert"), None),
        P(("dp", "expert")),
        P(("dp", "expert")),
        P(("dp", "expert"), None),
        P("expert", None, "dp"),
        P("expert", "dp", None),
        P(None, ("dp", "expert"), None, None),
    )
    return jax.shard_map(
        body,
        mesh=mesh,
        in_specs=placed,
        out_specs=(
            P(None, ("dp", "expert"), None, None),
            P(None, ("dp", "expert"), None, None),
            P(("dp", "expert")),
            P(("dp", "expert")),
            P(("dp", "expert"), None),
            P(("dp", "expert"), None),
            P(("dp", "expert")),
            P(("dp", "expert")),
            P(("dp", "expert"), None),
            P("expert", None, "dp"),
            P("expert", "dp", None),
        ),
        check_vma=False,
    )
```

profile of v0, /device:TPU:0, one launch (start us, length us, event | category | flops | bytes accessed | tf_op | source)
XLA Modules:
  0.0 1069.0 jit_solution(6583092266178322591)
XLA Ops:
  11.0 42.1 %all-reduce.22 = (bf16[768]{0:T(1024)(128)(2,1)S(1)}, bf16[768]{0:T(1024)(128)(2,1)S(1)}, bf16[768]{0:T(1024)(128)(2,1)S(1)}, bf16[768]{0:T(1024)(128)(2,1)S(1)}) all-reduce(bf16[768]{0:T(1024)(128)(2,1)S(1)} %dynamic-update-slice.1, bf16[768]{0:T(1024)(128)(2,1)S(1)} %dynamic-update-slice, ...), channel_id=1, replica_groups=mesh['dp'=8,'expert'=4] {'dp','expert'}, use_global_device_ids=true, to_apply=%add.13 | all-reduce | flops 3072 | bytes 12288
  59.2 41.0 %all-gather = bf16[32,24,8]{1,2,0:T(8,128)(2,1)S(1)} all-gather(bf16[1,24,8]{1,2,0:T(8,128)(2,1)S(1)} %bitcast.1096), channel_id=1, replica_groups=mesh['dp'=8,'expert'=4] {'dp','expert'}, dimensions={0}, use_global_device_ids=true | all-gather | bytes 12672 | tf_op jit(solution)/shard_map/all_gather | solution.py:119
  100.4 10.3 fusion.330
  126.9 6.2 convolution_convert_fusion.2
  138.6 6.1 convolution_convert_fusion.3
  144.7 6.0 copy.301
  150.7 5.9 convolution_convert_fusion.1
  293.0 114.2 %all-gather.12.cloned.1.call-done = bf16[2,3072,768]{2,1,0:T(8,128)(2,1)} async-done(((bf16[2,384,768]{2,1,0:T(8,128)(2,1)}), bf16[2,3072,768]{2,1,0:T(8,128)(2,1)}) %all-gather.12.cloned.1.call-update) | async-done | bytes 9437200 | tf_op jit(solution)/shard_map/all_gather | solution.py:124
  407.2 6.4 fusion.182
  413.6 7.9 fusion.261
  426.3 7.9 fusion.269
  438.2 7.9 fusion.265
  450.0 22.3 %add_convert_fusion.1 = bf16[2,768,3072]{2,1,0:T(8,128)(2,1)} fusion(f32[2,768,3072]{2,1,0:T(8,128)} %fusion.261, f32[2,768,3072]{2,1,0:T(8,128)} %fusion.269, f32[2,768,3072]{2,1,0:T(8,128)} %fusion.265, bf16[12,2,3072]{2,0,1:T(8,128)(2,1)S(1)} %fusion.174, bf16[12,2,768]{2,1,0:T(2,128)(2,1)S(1)} %bitcast.1065), kind=kOutput, calls=%fused_computation.1 | convolution fusion | flops 132120576 | bytes 66244608 | tf_op jit(solution)/shard_map/rsd,rsf->sdf/dot_general | solution.py:86
  472.3 23.8 %copy.449 = bf16[2,768,3072]{1,0,2:T(2,128)(2,1)} copy(bf16[2,768,3072]{2,1,0:T(8,128)(2,1)} %add_convert_fusion.1) | data formatting | bytes 18874368
  496.1 8.9 copy.471
  507.1 6.5 fusion.129
  517.5 6.3 fusion.128
  523.8 8.2 fusion.249
  532.0 8.8 fusion.255
  540.8 8.4 fusion.252
  556.9 23.1 %add_convert_fusion = bf16[2,3072,768]{2,1,0:T(8,128)(2,1)} fusion(f32[2,3072,768]{2,1,0:T(8,128)} %fusion.249, f32[2,3072,768]{2,1,0:T(8,128)} %fusion.255, f32[2,3072,768]{2,1,0:T(8,128)} %fusion.252, bf16[12,2,768]{2,1,0:T(2,128)(2,1)S(1)} %bitcast.1073, f32[2,12,3072]{2,1,0:T(8,128)S(1)} %fusion.259), kind=kOutput, calls=%fused_computation | convolution fusion | flops 136912896 | bytes 66392064 | tf_op jit(solution)/shard_map/rsf,rsd->sfd/dot_general | solution.py:85
  580.0 6.4 fusion.130
  590.8 6.4 fusion.131
  691.4 6.2 multiply_reduce_fusion.3
  701.6 11.7 %convert_reduce_fusion.2 = (f32[3,12,197]{2,1,0:T(8,128)S(1)}, pred[3,12,197,197]{2,3,1,0:T(8,128)(4,1)}, f32[3,12,197]{2,1,0:T(8,128)S(1)}, f32[3,12,197]{2,1,0...) fusion(f32[3,12,197]{2,1,0:T(8,128)S(1)} %copy-done.129, ...), kind=kLoop, calls=%fused_computation.20 | loop fusion | flops 25119864 | bytes 25431912 | tf_op jit(solution)/shard_map/jvp()/reduce_sum | solution.py:38
  713.3 5.9 add_convert_fusion.4
  748.8 11.7 %convert_reduce_fusion = (f32[3,12,197]{2,1,0:T(8,128)S(1)}, pred[3,12,197,197]{2,3,1,0:T(8,128)(4,1)}, f32[3,12,197]{2,1,0:T(8,128)S(1)}, f32[3,12,197]{2,1,0:T...) fusion(f32[3,12,197]{2,1,0:T(8,128)S(1)} %copy-done.125, f32[3,12,197,197]{2,3,1,0:T(8,128)S(1)} %bitcast.1004, ...), kind=kLoop, calls=%fused_computation.6 | loop fusion | flops 25119864 | bytes 25431912 | tf_op jit(solution)/shard_map/jvp()/reduce_sum | solution.py:38
  811.9 9.2 bitcast_add_fusion
  822.6 6.3 fusion.20
  847.9 39.3 %all-reduce.21 = (f32[768]{0:T(1024)S(1)}, f32[768]{0:T(1024)S(1)}, f32[768]{0:T(1024)S(1)}, f32[768]{0:T(1024)S(1)}, f32[768,8]{0,1:T(8,128)S(1)}) all-reduce(f32[768]{0:T(1024)S(1)} %add_add_fusion.11, f32[768]{0:T(1024)S(1)} %add_add_fusion.10, ...), channel_id=2, replica_groups=mesh['dp'=8,'expert'=4] {'dp','expert'}, use_global_device_ids=true, to_apply=%region_96.0.clone | all-reduce | flops 9216 | bytes 73728
  911.7 25.1 %reduce-scatter.10.cloned.1.call-done = f32[24,768]{1,0:T(8,128)} async-done(((f32[768,768]{1,0:T(8,128)}), f32[24,768]{1,0:T(8,128)}) %reduce-scatter.10.cloned.1.call-update) | async-done | bytes 73744 | tf_op jit(solution)/shard_map/reduce_scatter | solution.py:161
  936.8 125.2 %reduce-scatter.8.cloned.1.call-done = f32[24,2304]{1,0:T(8,128)} async-done(((f32[768,2304]{1,0:T(8,128)}), f32[24,2304]{1,0:T(8,128)}) %reduce-scatter.8.cloned.1.call-update) | async-done | bytes 221200 | tf_op jit(solution)/shard_map/reduce_scatter | solution.py:161
  (979 shorter events, 418.4 us)
Async XLA Ops:
  7.2 45.9 %copy-start.279 = (s32[4,1]{0,1:T(1,128)S(1)}, s32[4,1]{0,1:T(1,128)}, u32[]{:S(2)}) copy-start(s32[4,1]{0,1:T(1,128)} %param.13) | copy-start | bytes 52
  7.2 52.0 %copy-start.280 = (bf16[24,8]{0,1:T(8,128)(2,1)S(1)}, bf16[24,8]{0,1:T(8,128)(2,1)}, u32[]{:S(2)}) copy-start(bf16[24,8]{0,1:T(8,128)(2,1)} %param.20) | copy-start | bytes 1156
  7.2 119.7 %all-gather.6.cloned.1.call-start = ((), (), s32[]{:S(2)}) async-start(), calls=%async_computation.20 | async-start | bytes 3649536 | tf_op jit(solution)/shard_map/all_gather | solution.py:115
  8.0 202.7 %all-gather.8.cloned.1.call-start = ((), (), s32[]{:S(2)}) async-start(), calls=%async_computation.21 | async-start | bytes 1216512 | tf_op jit(solution)/shard_map/all_gather | solution.py:116
  8.7 279.2 %all-gather.10.cloned.1.call-start = ((), (), s32[]{:S(2)}) async-start(), calls=%async_computation.22 | async-start | bytes 10616832 | tf_op jit(solution)/shard_map/all_gather | solution.py:123
  9.5 397.7 %all-gather.12.cloned.1.call-start = ((), (), s32[]{:S(2)}) async-start(), calls=%async_computation.23 | async-start | bytes 10616832 | tf_op jit(solution)/shard_map/all_gather | solution.py:124
  58.6 55.2 %copy-start.155 = (f32[768]{0:T(1024)}, f32[768]{0:T(1024)S(1)}, u32[]{:S(2)}) copy-start(f32[768]{0:T(1024)S(1)} %convert_element_type.550) | copy-start | bytes 9220
  100.4 147.1 %copy-start.135 = (bf16[768,8,1]{0,1,2:T(8,128)(2,1)}, bf16[768,8,1]{0,1,2:T(8,128)(2,1)S(1)}, u32[]{:S(2)}) copy-start(bf16[768,8,1]{0,1,2:T(8,128)(2,1)S(1)} %reshape.554) | copy-start | bytes 36868
  186.8 319.6 %copy-start.130 = (f32[3,12,197]{2,1,0:T(8,128)}, f32[3,12,197]{2,1,0:T(8,128)S(1)}, u32[]{:S(2)}) copy-start(f32[3,12,197]{2,1,0:T(8,128)S(1)} %fusion.30) | copy-start | bytes 85108
  225.6 51.0 %copy-start.52 = (bf16[3,197,768]{2,1,0:T(8,128)(2,1)}, bf16[3,197,768]{2,1,0:T(8,128)(2,1)S(1)}, u32[]{:S(2)}) copy-start(bf16[3,197,768]{2,1,0:T(8,128)(2,1)S(1)} %get-tuple-element.201) | copy-start | bytes 2723332
  226.3 278.8 %copy-start.233 = (f32[3,8]{1,0:T(4,128)}, f32[3,8]{1,0:T(4,128)S(1)}, u32[]{:S(2)}) copy-start(f32[3,8]{1,0:T(4,128)S(1)} %get-tuple-element.99) | copy-start | bytes 292
  227.3 277.7 %copy-start.231 = (f32[3,8]{1,0:T(4,128)}, f32[3,8]{1,0:T(4,128)S(1)}, u32[]{:S(2)}) copy-start(f32[3,8]{1,0:T(4,128)S(1)} %get-tuple-element.107) | copy-start | bytes 292
  229.6 7.3 all-to-all-start.14
  236.9 7.3 all-to-all-start.6
  244.1 7.3 all-to-all-start.12
  251.4 7.3 all-to-all-start.4
  258.7 7.3 all-to-all-start.8
  266.0 7.3 all-to-all-start
  273.3 7.3 all-to-all-start.10
  280.6 7.3 all-to-all-start.2
  283.9 618.5 %reduce-scatter.14.cloned.1.call-start = ((), (), s32[]{:S(2)}) async-start(), calls=%async_computation.27 | async-start | bytes 10616832
  514.2 72.8 %all-to-all-start.11 = ((bf16[12,2,768]{2,1,0:T(2,128)(2,1)}), bf16[12,2,768]{2,1,0:T(2,128)(2,1)S(1)}, u32[]{:S(2)}, u32[]{:S(2)}) async-start(bf16[12,2,768]{2,1,0:T(2,128)(2,1)} %copy.365), calls=%async_computation.11 | async-start | bytes 73728 | tf_op jit(solution)/shard_map/all_to_all | solution.py:150
  587.0 14.1 %all-to-all-start.9 = ((bf16[12,2,768]{2,1,0:T(2,128)(2,1)}), bf16[12,2,768]{2,1,0:T(2,128)(2,1)S(1)}, u32[]{:S(2)}, u32[]{:S(2)}) async-start(bf16[12,2,768]{2,1,0:T(2,128)(2,1)} %copy.353), calls=%async_computation.9 | async-start | bytes 73728 | tf_op jit(solution)/shard_map/all_to_all | solution.py:150
  590.3 318.5 %reduce-scatter.12.cloned.1.call-start = ((), (), s32[]{:S(2)}) async-start(), calls=%async_computation.26 | async-start | bytes 10616832 | tf_op jit(solution)/shard_map/reduce_scatter | solution.py:166
  601.1 7.2 all-to-all-start.13
  608.4 7.4 all-to-all-start.15
  615.8 7.2 all-to-all-start.3
  623.0 7.2 all-to-all-start.1
  630.2 7.2 all-to-all-start.5
  637.4 7.7 all-to-all-start.7
  640.7 296.1 %reduce-scatter.10.cloned.1.call-start = ((), (), s32[]{:S(2)}) async-start(), calls=%async_computation.25 | async-start | bytes 2433024 | tf_op jit(solution)/shard_map/reduce_scatter | solution.py:161
  795.7 266.2 %reduce-scatter.8.cloned.1.call-start = ((), (), s32[]{:S(2)}) async-start(), calls=%async_computation.24 | async-start | bytes 7299072 | tf_op jit(solution)/shard_map/reduce_scatter | solution.py:161
  (300 other events, 1757.8 us)
Sparse Core Ops, SparseCore 0:
  11.0 62.7 all-gather.5
  76.7 52.8 all-gather.7
  131.7 137.1 all-gather.9
  270.9 136.2 all-gather.11
  505.2 161.4 reduce-scatter.13
  670.1 162.5 reduce-scatter.11
  838.6 98.1 reduce-scatter.9
  943.9 117.9 reduce-scatter.7
where the time goes:
time: 1080 us; the launch traced here: 1070 us
  matrix products  309 us (29%)
  waiting for transfers between devices  297 us (28%)
  local copies, waits for them, and re-layouts  162 us (15%)
  blocking collectives  122 us (11%)
  other arithmetic  106 us (10%)
  starting transfers between devices  53.9 us (5%)
  between operations  18.9 us (2%)
    reduce_scatter x2, waiting for transfers between devices, body(): lax.psum_scatter(dense_sums, ('dp', 'expert'), scatter_dimension=0, tiled...  150 us
    all_gather x1, waiting for transfers between devices, body(): lax.all_gather(w_down, 'dp', axis=1, tiled=True)  114 us
    unnamed x640, local copies, waits for them, and re-layouts  98.6 us
    unnamed x2, blocking collectives  81.5 us
    dot_general x12, matrix products, mixer_part(): triple = back_rounded(rounded(jnp.einsum('gtd,de->gte', normed, w_qkv)))  66.4 us
    dot_general x4, matrix products, expert_backward(): jnp.einsum('rsf,rsd->sfd', active, grad_out, preferred_element_type=jnp.f...  48.6 us
    dot_general x4, matrix products, expert_backward(): jnp.einsum('rsd,rsf->sdf', slot_rows, grad_pre, preferred_element_type=jn...  46.1 us
    all_gather x1, blocking collectives, body(): lax.all_gather(phi, ('dp', 'expert'), axis=0, tiled=True)  41 us
  transfers between devices with their start and end apart: 24, of which 14 were waited for; matrix products, arithmetic and copies ran while one was open for 41% of the time, Pallas kernels for 0%

commit v1 on v0

v1 whole, which is shorter than its diff:
```python
from functools import partial

import jax
import jax.numpy as jnp
from jax import lax
from jax.sharding import PartitionSpec as P

HEADS = 12
HEAD_DIM = 64
EPSILON = 1e-06
BOTH = ("dp", "expert")


class Grid:
    def __init__(self, n, m):
        self.n, self.m = n, m
        self.size = {"z": n // 2, "y": 2, "x": m // 2, "c": 2}

    def coords(self):
        d, e = lax.axis_index("dp"), lax.axis_index("expert")
        return {"z": d // 2, "y": d % 2, "x": e // 2, "c": e % 2}

    def perm(self, axis, k):
        pairs = []
        for z in range(self.size["z"]):
            for y in range(2):
                for x in range(self.size["x"]):
                    for c in range(2):
                        p = {"z": z, "y": y, "x": x, "c": c}
                        q = dict(p)
                        q[axis] = (q[axis] + k) % self.size[axis]
                        pairs.append(tuple((r["z"] * 2 + r["y"]) * self.m + r["x"] * 2 + r["c"] for r in (p, q)))
        return pairs

    def send(self, a, axis, k):
        return lax.ppermute(a, BOTH, self.perm(axis, k))

    def by_coordinate(self, me, axis, pieces):
        s = self.size[axis]
        if s == 2:
            return jnp.stack([jnp.where(me == p, pieces[0], pieces[1]) for p in range(2)])
        if s <= 4:
            return jnp.stack([lax.select_n((me - p) % s, *pieces) for p in range(s)])
        out = jnp.zeros((s,) + pieces[0].shape, pieces[0].dtype)
        for k in range(s):
            out = lax.dynamic_update_index_in_dim(out, pieces[k], (me - k) % s, 0)
        return out

    def gather(self, a, axis, me):
        pieces = [a] + [self.send(a, axis, k) for k in range(1, self.size[axis])]
        return self.by_coordinate(me[axis], axis, pieces)

    def block(self, a, axis, me, k):
        return lax.dynamic_index_in_dim(a, (me[axis] + k) % self.size[axis], 0, keepdims=False)

    def scatter_sum(self, a, axis, me):
        own = self.block(a, axis, me, 0).astype(jnp.float32)
        for k in range(1, self.size[axis]):
            own = own + self.send(self.block(a, axis, me, k), axis, k).astype(jnp.float32)
        return own

    def exchange(self, a, axis, me):
        pieces = [self.block(a, axis, me, k) for k in range(self.size[axis])]
        pieces = pieces[:1] + [self.send(p, axis, k) for k, p in enumerate(pieces) if k]
        return self.by_coordinate(me[axis], axis, pieces)


def joined(parts, axis):
    return jnp.concatenate(parts, axis=axis) if len(parts) > 1 else parts[0]


def gather_rows(grid, a, cuts, me):
    outs, low = [], 0
    for width, order in cuts:
        b, done = a[:, low : low + width], []
        low += width
        for axis in order:
            b = grid.gather(b, axis, me)
            done.insert(0, axis)
        outs.append(jnp.transpose(b, [done.index(axis) for axis in "zyxc"] + [4, 5]))
    return joined(outs, -1).reshape(-1, a.shape[1])


def reduce_rows(grid, a, cuts, me):
    s = grid.size
    a = a.reshape(s["z"], 2, s["x"], 2, -1, a.shape[1])
    outs, low = [], 0
    for width, order in cuts:
        b, left = a[..., low : low + width], ["z", "y", "x", "c"]
        low += width
        for axis in order:
            b = jnp.moveaxis(b.astype(jnp.bfloat16), left.index(axis), 0)
            b = grid.scatter_sum(b, axis, me)
            left.remove(axis)
        outs.append(b)
    return joined(outs, -1)


def to_experts(grid, a, part, me):
    s = grid.size
    b = grid.exchange(a.reshape(s["x"], 2, *a.shape[1:]), "x", me)
    b = grid.exchange(jnp.moveaxis(b, 1, 0), "c", me)
    b = jnp.moveaxis(b, 0, 1).reshape(a.shape)
    first = grid.gather(grid.gather(b[:, :part], "z", me), "y", me)
    second = grid.gather(grid.gather(b[:, part:], "y", me), "z", me)
    r = jnp.concatenate([jnp.moveaxis(first, 0, 1), second], axis=3)
    return r.reshape(grid.n, *a.shape)


def from_experts(grid, a, part, me):
    s = grid.size
    b = a.reshape(s["z"], 2, *a.shape[1:])
    first = grid.scatter_sum(jnp.moveaxis(b[:, :, :, :part], 1, 0), "y", me).astype(jnp.bfloat16)
    first = grid.scatter_sum(first, "z", me)
    second = grid.scatter_sum(b[:, :, :, part:], "z", me).astype(jnp.bfloat16)
    second = grid.scatter_sum(second, "y", me)
    r = jnp.concatenate([first, second], axis=1).astype(jnp.bfloat16)
    r = grid.exchange(r.reshape(s["x"], 2, *r.shape[1:]), "x", me)
    r = grid.exchange(jnp.moveaxis(r, 1, 0), "c", me)
    return jnp.moveaxis(r, 0, 1).reshape(a.shape[1:])


def round_down(v):
    return lax.optimization_barrier(v.astype(jnp.bfloat16)).astype(jnp.float32)


def same_value(v):
    return v


def make_rounders():
    rounded = jax.custom_vjp(round_down)
    rounded.defvjp(lambda v: (round_down(v), None), lambda kept, grad: (grad,))
    back_rounded = jax.custom_vjp(same_value)
    back_rounded.defvjp(lambda v: (v, None), lambda kept, grad: (round_down(grad),))
    return (rounded, back_rounded)


def normalize(values, norm_gain, norm_bias):
    center = values - jnp.mean(values, axis=-1, keepdims=True)
    spread = jnp.mean(center * center, axis=-1, keepdims=True)
    return center * lax.rsqrt(spread + EPSILON) * norm_gain + norm_bias


def softmax_along(values, dimension):
    largest = jnp.max(values, axis=dimension, keepdims=True)
    powers = jnp.exp(values - largest)
    return powers / jnp.sum(powers, axis=dimension, keepdims=True)


def mixer_part(inputs, ln1_gain, ln1_bias, w_qkv, w_out, ln2_gain, ln2_bias, phi):
    rounded, back_rounded = make_rounders()
    images, length, features = inputs.shape
    normed = rounded(normalize(inputs, ln1_gain, ln1_bias))
    triple = back_rounded(rounded(jnp.einsum("gtd,de->gte", normed, w_qkv)))
    triple = triple.reshape(images, length, 3, HEADS, HEAD_DIM)
    queries = triple[:, :, 0]
    keys_all = triple[:, :, 1]
    values_all = triple[:, :, 2]
    scores = back_rounded(jnp.einsum("gqhc,gkhc->ghqk", queries, keys_all) * HEAD_DIM ** (-0.5))
    attention = rounded(softmax_along(scores, 3))
    mixed_heads = jnp.einsum("ghqk,gkhc->gqhc", attention, values_all)
    mixed_heads = back_rounded(rounded(mixed_heads.reshape(images, length, features)))
    branch = back_rounded(jnp.einsum("gtd,de->gte", mixed_heads, w_out))
    hidden_state = inputs + branch
    normed_two = rounded(normalize(hidden_state, ln2_gain, ln2_bias))
    logits = back_rounded(jnp.einsum("gtd,ds->gts", normed_two, phi))
    dispatch = rounded(softmax_along(logits, 1))
    combine = rounded(softmax_along(logits, 2))
    slot_in = back_rounded(rounded(jnp.einsum("gts,gtd->gsd", dispatch, normed_two)))
    return (hidden_state, combine, slot_in)


def combine_part(hidden_state, combine, slot_out):
    rounded, back_rounded = make_rounders()
    slot_out = back_rounded(slot_out)
    return hidden_state + jnp.einsum("gts,gsd->gtd", combine, slot_out)


def experts(rows, grads, up, down):
    f32 = jnp.float32
    pre = jnp.einsum("rsd,sdf->srf", rows, up, preferred_element_type=f32)
    active, slope = jax.vjp(partial(jax.nn.gelu, approximate=False), pre)
    active = active.astype(jnp.bfloat16)
    out = jnp.einsum("srf,sfd->rsd", active, down, preferred_element_type=f32)
    grad_active = jnp.einsum("rsd,sfd->srf", grads, down, preferred_element_type=f32)
    grad_pre = slope(grad_active)[0].astype(jnp.bfloat16)
    grad_rows = jnp.einsum("srf,sdf->rsd", grad_pre, up, preferred_element_type=f32)
    grad_up = jnp.einsum("rsd,srf->sdf", rows, grad_pre, preferred_element_type=f32)
    grad_down = jnp.einsum("srf,rsd->sfd", active, grads, preferred_element_type=f32)
    return (out, grad_rows, grad_up, grad_down)


def body(grid, inputs, counts, ln1_gain, ln1_bias, w_qkv, w_out, ln2_gain, ln2_bias, phi, w_up, w_down, cotangent):
    me = grid.coords()
    batches, capacity, length, features = inputs.shape
    images = batches * capacity
    slots = phi.shape[1]
    per = slots // grid.m
    vectors = jnp.stack([ln1_gain, ln1_bias, ln2_gain, ln2_bias], axis=1)
    small = jnp.concatenate([vectors, phi], axis=1)
    small = jnp.pad(small, ((0, 0), (0, 128 - small.shape[1])))
    packed = jnp.concatenate([w_qkv, w_out, small], axis=1)
    whole = gather_rows(grid, packed, ((1664, "zyxc"), (1536, "zxyc")), me)
    w_qkv_all, w_out_all = whole[:, : 3 * features], whole[:, 3 * features : 4 * features]
    small_all = whole[:, 4 * features :]
    dense = (
        small_all[:, 0],
        small_all[:, 1],
        w_qkv_all,
        w_out_all,
        small_all[:, 2],
        small_all[:, 3],
        small_all[:, 4 : 4 + slots],
    )
    dense = tuple(member.astype(jnp.float32) for member in dense)
    live = (jnp.arange(capacity)[None, :] < counts).astype(jnp.float32).reshape(images, 1, 1)
    image_in = inputs.reshape(images, length, features).astype(jnp.float32)
    (hidden_state, combine, slot_in), mixer_back = jax.vjp(mixer_part, image_in, *dense)
    grad_result = cotangent.reshape(images, length, features).astype(jnp.float32) * live
    grad_slot = jnp.einsum("gts,gtd->gsd", combine, grad_result)
    leaving = jnp.stack([slot_in.astype(jnp.bfloat16), grad_slot.astype(jnp.bfloat16)])
    leaving = leaving.reshape(2 * images, grid.m, per * features).transpose(1, 0, 2)
    rows_all = 2 * images
    arrived = to_experts(grid, leaving, rows_all * 2 // 3, me)
    arrived = arrived.reshape(grid.n * grid.m, 2, images, per, features)
    rows = arrived[:, 0].reshape(-1, per, features)
    grads = arrived[:, 1].reshape(-1, per, features)
    out, grad_rows, grad_up, grad_down = experts(rows, grads, w_up, w_down)
    back = jnp.stack([out.astype(jnp.bfloat16).reshape(-1, images, per * features), grad_rows.astype(jnp.bfloat16).reshape(-1, images, per * features)], axis=1)
    back = back.reshape(grid.n, grid.m, rows_all, per * features)
    home = from_experts(grid, back, rows_all * 2 // 3, me)
    home = home.transpose(1, 0, 2).reshape(2, images, slots, features).astype(jnp.float32)
    result, combine_back = jax.vjp(combine_part, hidden_state, combine, home[0])
    output = (result * live).astype(jnp.bfloat16)
    grad_hidden, grad_combine, _ = combine_back(grad_result)
    grads_all = mixer_back((grad_hidden, grad_combine, home[1]))
    vectors = jnp.stack([grads_all[1], grads_all[2], grads_all[5], grads_all[6]], axis=1)
    small = jnp.concatenate([vectors, grads_all[7]], axis=1)
    small = jnp.pad(small, ((0, 0), (0, 128 - small.shape[1])))
    packed = jnp.concatenate([grads_all[3], grads_all[4], small], axis=1)
    sums = reduce_rows(grid, packed, ((1664, "cxyz"), (1536, "cyxz")), me)
    small = sums[:, 4 * features :]
    return (
        output.reshape(inputs.shape),
        grads_all[0].astype(jnp.bfloat16).reshape(inputs.shape),
        small[:, 0],
        small[:, 1],
        sums[:, : 3 * features],
        sums[:, 3 * features : 4 * features],
        small[:, 2],
        small[:, 3],
        small[:, 4 : 4 + slots],
        grad_up,
        grad_down,
    )


def solution(mesh):
    rows = P(BOTH, None)
    row = P(BOTH)
    image = P(None, BOTH, None, None)
    up, down = P("expert", None, "dp"), P("expert", "dp", None)
    grid = Grid(mesh.shape["dp"], mesh.shape["expert"])
    return jax.shard_map(
        partial(body, grid),
        mesh=mesh,
        in_specs=(image, P(None, BOTH), row, row, rows, rows, row, row, rows, up, down, image),
        out_specs=(image, image, row, row, rows, rows, row, row, rows, up, down),
        check_vma=False,
    )
```

time: 1080 us -> 619 us (0.57)
  waiting for transfers between devices: 297 us -> 108 us
  matrix products: 309 us -> 185 us
  blocking collectives: 122 us -> 0 us
  local copies, waits for them, and re-layouts: 162 us -> 106 us
  other arithmetic: 106 us -> 148 us
  between operations: 18.9 us -> 2.8 us
    reduce_scatter x3 -> x0, waiting for transfers between devices: 150 us -> none  [the longest x2 150 us: body(): lax.psum_scatter(dense_sums, ('dp', 'expert'), scatter_dimension=0, tiled...]
    dot_general x24 -> x7, matrix products: 151 us -> 11.3 us  [the longest x1 3.32 us: experts(): jnp.einsum('rsd,sfd->srf', grads, down, preferred_element_type=f32)]
    all_gather x4 -> x0, waiting for transfers between devices: 114 us -> none  [the longest x1 114 us: body(): lax.all_gather(w_down, 'dp', axis=1, tiled=True)]
    ppermute x0 -> x44, waiting for transfers between devices: none -> 108 us  [send(): return lax.ppermute(a, BOTH, self.perm(axis, k))]
    unnamed x2 -> x0, blocking collectives: 81.5 us -> none
    unnamed x640 -> x179, local copies, waits for them, and re-layouts: 98.6 us -> 31.8 us
    ppermute x0 -> x44, starting transfers between devices: none -> 62.2 us  [send(): return lax.ppermute(a, BOTH, self.perm(axis, k))]
    all_to_all x16 -> x0, starting transfers between devices: 52.5 us -> none  [the longest x4 13.2 us: body(): lax.all_to_all(grad_rows.astype(jnp.bfloat16), 'expert', split_axis=0, co...]
  transfers between devices with their start and end apart: 24 -> 44, of which waited for: 14 -> 27; matrix products, arithmetic and copies ran while one was open for 41% -> 10% of each run, Pallas kernels for 0% -> 0%
where the time goes in v1:
time: 619 us; the launch traced here: 611 us
  matrix products  185 us (30%)
  other arithmetic  148 us (24%)
  waiting for transfers between devices  108 us (17%)
  local copies, waits for them, and re-layouts  106 us (17%)
  starting transfers between devices  62.2 us (10%)
    ppermute x44, waiting for transfers between devices, send(): return lax.ppermute(a, BOTH, self.perm(axis, k))  108 us
    ppermute x44, starting transfers between devices, send(): return lax.ppermute(a, BOTH, self.perm(axis, k))  62.2 us
    dot_general x3, matrix products, mixer_part(): mixed_heads = jnp.einsum('ghqk,gkhc->gqhc', attention, values_all)  49.4 us
    dot_general x3, matrix products, mixer_part(): triple = back_rounded(rounded(jnp.einsum('gtd,de->gte', normed, w_qkv)))  43.8 us
    dot_general x3, matrix products, mixer_part(): jnp.einsum('gqhc,gkhc->ghqk', queries, keys_all) * HEAD_DIM ** (-0.5)  36 us
    unnamed x179, local copies, waits for them, and re-layouts  31.8 us
    convert_element_type x1, other arithmetic, mixer_part(): back_rounded(jnp.einsum('gqhc,gkhc->ghqk', queries, keys_all) * HEAD_DIM...  28.1 us
    reduce_sum x1, other arithmetic, softmax_along(): largest = jnp.max(values, axis=dimension, keepdims=True)  26.9 us
  transfers between devices with their start and end apart: 44, of which 27 were waited for; matrix products, arithmetic and copies ran while one was open for 10% of the time, Pallas kernels for 0%

profile of v1, /device:TPU:0, one launch (start us, length us, event | category | flops | bytes accessed | tf_op | source)
XLA Modules:
  0.0 611.3 jit_solution(960964219321980726)
XLA Ops:
  36.6 7.6 %collective-permute-done.3 = bf16[4,24,1664]{2,1,0:T(8,128)(2,1)S(1)} collective-permute-done((bf16[4,24,1664]{2,1,0:T(8,128)(2,1)S(1)}, bf16[4,24,1664]{2,1,0:T(8,128)(2,1)S(1)}, u32[]{:S(2)}, u32[]{:S(2)}) %collective-permute-start.3) | collective-permute-done | bytes 319520 | tf_op jit(solution)/shard_map/ppermute | solution.py:36
  45.9 7.2 %collective-permute-done.10 = bf16[2,4,24,1536]{3,2,1,0:T(8,128)(2,1)S(1)} collective-permute-done((bf16[2,4,24,1536]{3,2,1,0:T(8,128)(2,1)S(1)}, bf16[2,4,24,1536]{3,2,1,0:T(8,128)(2,1)S(1)}, u32[]{:S(2)}, u32[]{:S(2)}) %collective-permute-start.10) | collective-permute-done | bytes 589856 | tf_op jit(solution)/shard_map/ppermute | solution.py:36
  62.2 6.7 %bitcast_multiply_fusion = f32[12,197,768]{2,1,0:T(8,128)} fusion(f32[4,3,197,768]{3,2,1,0:T(8,128)} %copy.329, f32[12]{0:T(128)S(1)} %reshape.325), kind=kLoop, calls=%fused_computation.21 | loop fusion | flops 1815552 | bytes 14524464 | tf_op jit(solution)/shard_map/mul | solution.py:220
  80.6 11.2 %convolution_convert_fusion = bf16[12,197,2304]{2,1,0:T(8,128)(2,1)} fusion(bf16[12,197,768]{2,1,0:T(8,128)(2,1)S(1)} %add_convert_fusion.4, bf16[768,3200]{1,0:T(8,128)(2,1)S(1)} %bitcast.406), kind=kOutput, calls=%fused_computation.20 | convolution fusion | flops 8371510272 | bytes 18118656 | tf_op jit(solution)/shard_map/jvp(gtd,de->gte)/dot_general | solution.py:155
  91.8 16.4 %copy.322 = bf16[12,197,2304]{1,2,0:T(8,128)(2,1)} copy(bf16[12,197,2304]{2,1,0:T(8,128)(2,1)} %convolution_convert_fusion) | data formatting | bytes 21786624 | tf_op jit(solution)/shard_map/jvp()/optimization_barrier | solution.py:124
  108.2 14.2 %multiply_reduce_fusion.1 = (f32[12,12,197]{2,1,0:T(8,128)S(1)}, f32[12,12,197,197]{2,3,1,0:T(8,128)}) fusion(bf16[12,197,3,12,64]{1,4,3,2,0:T(8,128)(2,1)} %bitcast.386), kind=kOutput, calls=%fused_computation.11 | convolution fusion | flops 726476096 | bytes 31904640 | tf_op jit(solution)/shard_map/jvp(gqhc,gkhc->ghqk)/dot_general | solution.py:160
  122.5 10.6 %fusion.4 = f32[12,12,197]{2,1,0:T(8,128)S(1)} fusion(f32[12,12,197]{2,1,0:T(8,128)S(1)} %get-tuple-element.189, f32[12,12,197,197]{2,3,1,0:T(8,128)} %get-tuple-element.190), kind=kLoop, calls=%fused_computation.14 | loop fusion | flops 16737120 | bytes 22580928 | tf_op jit(solution)/shard_map/jvp()/reduce_sum | solution.py:148
  133.1 7.2 %copy-done.2 = f32[12,12,197,197]{2,3,1,0:T(8,128)S(1)} copy-done((f32[12,12,197,197]{2,3,1,0:T(8,128)S(1)}, f32[12,12,197,197]{2,3,1,0:T(8,128)}, u32[]{:S(2)}) %copy-start.2) | copy-done | bytes 22354008
  140.4 9.4 %divide_convert_fusion = bf16[12,12,197,197]{2,3,1,0:T(8,128)(2,1)} fusion(f32[12,12,197]{2,1,0:T(8,128)S(1)} %fusion.4, f32[12,12,197]{2,1,0:T(8,128)S(1)} %get-tuple-element.189, f32[12,12,197,197]{2,3,1,0:T(8,128)S(1)} %copy-done.2), kind=kLoop, calls=%fused_computation.7 | loop fusion | flops 22353984 | bytes 33757920 | tf_op jit(solution)/shard_map/jvp()/convert_element_type | solution.py:124
  149.7 11.8 %fusion.11 = bf16[12,12,64,197]{3,2,1,0:T(8,128)(2,1)} fusion(bf16[12,12,197,197]{2,3,1,0:T(8,128)(2,1)} %divide_convert_fusion, bf16[12,197,3,12,64]{1,4,3,2,0:T(8,128)(2,1)} %bitcast.387), kind=kOutput, calls=%fused_computation.48 | convolution fusion | flops 717143040 | bytes 23095296 | tf_op jit(solution)/shard_map/jvp(ghqk,gkhc->gqhc)/dot_general | solution.py:162
  161.6 6.1 %fusion.82 = (f32[12,197]{1,0:T(8,128)S(1)}, f32[12,197,768]{2,1,0:T(8,128)S(1)}) fusion(f32[12,197,768]{2,1,0:T(8,128)S(1)} %bitcast.381, bf16[12,197,768]{1,2,0:T(8,128)(2,1)} %bitcast.403, bf16[768,3200]{1,0:T(8,128)(2,1)} %bitcast.407), kind=kOutput, calls=%fused_computation.286 | convolution fusion | flops 2792316672 | bytes 20432112 | tf_op jit(solution)/shard_map/jvp(gtd,de->gte)/dot_general | solution.py:164
  194.7 11.3 %collective-permute-done.15 = bf16[4,16,1536]{2,1,0:T(8,128)(2,1)S(1)} collective-permute-done((bf16[4,16,1536]{2,1,0:T(8,128)(2,1)S(1)}, bf16[4,16,1536]{2,1,0:T(8,128)(2,1)S(1)}, u32[]{:S(2)}, u32[]{:S(2)}) %collective-permute-start.15) | collective-permute-done | bytes 196640 | tf_op jit(solution)/shard_map/ppermute | solution.py:36
  206.8 12.5 %collective-permute-done.20 = bf16[2,4,8,1536]{3,2,1,0:T(8,128)(2,1)S(1)} collective-permute-done((bf16[2,4,8,1536]{3,2,1,0:T(8,128)(2,1)S(1)}, bf16[2,4,8,1536]{3,2,1,0:T(8,128)(2,1)S(1)}, u32[]{:S(2)}, u32[]{:S(2)}) %collective-permute-start.20) | collective-permute-done | bytes 196640 | tf_op jit(solution)/shard_map/ppermute | solution.py:36
  265.8 11.5 %collective-permute-start.26 = (bf16[2,4,8,1536]{3,1,0,2:T(4,128)(2,1)S(1)}, bf16[2,4,8,1536]{3,1,0,2:T(4,128)(2,1)S(1)}, u32[]{:S(2)}, u32[]{:S(2)}) collective-permute-start(bf16[2,4,8,1536]{3,1,0,2:T(4,128)(2,1)S(1)} %get-tuple-element.142), channel_id=1, source_target_pairs={{0,8},{1,9},{2,10},{3,11},{4,12},{5,13},{6,14},{7,15},{8,16},{9,17... | collective-permute-start | bytes 589832 | tf_op jit(solution)/shard_map/ppermute | solution.py:36
  285.1 6.2 %collective-permute-done.27 = bf16[2,4,8,1536]{3,1,0,2:T(4,128)(2,1)S(1)} collective-permute-done((bf16[2,4,8,1536]{3,1,0,2:T(4,128)(2,1)S(1)}, bf16[2,4,8,1536]{3,1,0,2:T(4,128)(2,1)S(1)}, u32[]{:S(2)}, u32[]{:S(2)}) %collective-permute-start.27) | collective-permute-done | bytes 196640 | tf_op jit(solution)/shard_map/ppermute | solution.py:36
  292.2 6.2 %collective-permute-done.22 = bf16[4,4,16,1536]{3,1,0,2:T(4,128)(2,1)S(1)} collective-permute-done((bf16[4,4,16,1536]{3,1,0,2:T(4,128)(2,1)S(1)}, bf16[4,4,16,1536]{3,1,0,2:T(4,128)(2,1)S(1)}, u32[]{:S(2)}, u32[]{:S(2)}) %collective-permute-start.22) | collective-permute-done | bytes 786464 | tf_op jit(solution)/shard_map/ppermute | solution.py:36
  308.3 6.3 %collective-permute-done.24 = bf16[4,16,1536]{2,0,1:T(4,128)(2,1)S(1)} collective-permute-done((bf16[4,16,1536]{2,0,1:T(4,128)(2,1)S(1)}, bf16[4,16,1536]{2,0,1:T(4,128)(2,1)S(1)}, u32[]{:S(2)}, u32[]{:S(2)}) %collective-permute-start.24) | collective-permute-done | bytes 196640 | tf_op jit(solution)/shard_map/ppermute | solution.py:36
  336.8 7.4 %multiply_reduce_fusion.2 = (bf16[768]{0:T(1024)(128)(2,1)}, f32[12,197]{1,0:T(8,128)S(1)}, bf16[768]{0:T(1024)(128)(2,1)}, f32[12,197,768]{2,1,0:T(8,128)S(1)}) fusion(f32[12,197,768]{2,1,0:T(8,128)} %copy-done.3, f32[12,197]{1,0:T(8,128)S(1)} %copy-done.49, f32[12,197]{1,0:T(8,128)S(1)} %copy-done.39, f32[768]{0:T(1024)S(1)} %copy-done.62, ...), kind=kOutput, calls=%fused_computation.22 | convolution fusion | flops 45384900 | bytes 22166160 | tf_op jit(solution)/shard_map/transpose(jvp(gtd,ds->gts))/dot_general | solution.py:167
  350.1 6.8 %convolution_bitcast_fusion.2 = bf16[768,768]{1,0:T(8,128)(2,1)} fusion(bf16[12,197,768]{1,2,0:T(8,128)(2,1)} %bitcast.404, bf16[12,197,768]{2,1,0:T(8,128)(2,1)S(1)} %fusion.12), kind=kOutput, calls=%fused_computation.61 | convolution fusion | flops 2788687872 | bytes 8441856 | tf_op jit(solution)/shard_map/transpose(jvp(gtd,de->gte))/dot_general | solution.py:164
  356.9 5.9 convolution_convert_fusion.1
  362.8 6.3 %copy.347 = bf16[12,197,768]{1,2,0:T(8,128)(2,1)} copy(bf16[12,197,768]{2,1,0:T(8,128)(2,1)} %convolution_convert_fusion.1) | data formatting | bytes 7262208 | tf_op jit(solution)/shard_map/transpose(jvp())/optimization_barrier | solution.py:163
  369.1 11.4 %convolution_bitcast_fusion.1 = f32[12,197,1,12,64]{1,4,3,0,2:T(8,128)} fusion(bf16[12,12,64,197]{3,2,1,0:T(8,128)(2,1)} %bitcast.393, bf16[12,12,197,197]{2,3,1,0:T(8,128)(2,1)} %divide_convert_fusion), kind=kOutput, calls=%fused_computation.45 | convolution fusion | flops 715327488 | bytes 22070304 | tf_op jit(solution)/shard_map/transpose(jvp(ghqk,gkhc->gqhc))/dot_general | solution.py:162
  380.5 26.2 %multiply_reduce_fusion = (f32[12,12,197]{2,1,0:T(8,128)S(1)}, f32[12,12,197,197]{2,3,1,0:T(8,128)}) fusion(f32[12,12,197]{2,1,0:T(8,128)S(1)} %copy-done.29, f32[12,12,197]{2,1,0:T(8,128)S(1)} %copy-done.11, f32[12,12,197,197]{2,3,1,0:T(8,128)} %get-tuple-element.190, bf16[12,12,64,197]{3,2,1,0:T(8,128)(2,1)} %bitcast.394, ...), kind=kOutput, calls=%fused_computation.6 | convolution fusion | flops 743241536 | bytes 61622784 | tf_op jit(solution)/shard_map/transpose(jvp(ghqk,gkhc->gqhc))/dot_general | solution.py:162
  406.7 26.9 %convert_reduce_fusion = (f32[12,12,197]{2,1,0:T(8,128)S(1)}, pred[12,12,197,197]{2,3,1,0:T(8,128)(4,1)}, f32[12,12,197]{2,1,0:T(8,128)S(1)}) fusion(f32[12,12,197]{2,1,0:T(8,128)S(1)} %copy-done.11, f32[12,12,197,197]{2,3,1,0:T(8,128)} %get-tuple-element.190, f32[12,12,197]{2,1,0:T(8,128)S(1)} %neg.47, f32[12,12,197,197]{2,3,1,0:T(8,128)} %get-tuple-element.198, ...), kind=kLoop, calls=%fused_computation.4 | loop fusion | flops 50239728 | bytes 50863824 | tf_op jit(solution)/shard_map/jvp()/reduce_sum | solution.py:146
  433.7 28.1 %add_convert_fusion = bf16[12,12,197,197]{2,3,1,0:T(8,128)(2,1)} fusion(pred[12,12,197,197]{2,3,1,0:T(8,128)(4,1)} %get-tuple-element.120, f32[12,12,197]{2,1,0:T(8,128)S(1)} %negate_divide_fusion, f32[12,12,197]{2,1,0:T(8,128)S(1)} %copy-done.11, f32[12,12,197,197]{2,3,1,0:T(8,128)} %get-tuple-element.190, f32[12,12,197]{2,1,0:T(8,128)S(1)} %neg.47, ...), kind=kLoop, calls=%fused_computation.3 | loop fusion | flops 44707968 | bytes 61927344 | tf_op jit(solution)/shard_map/transpose(jvp())/convert_element_type | solution.py:160
  461.8 10.7 %fusion.10 = f32[12,197,1,12,64]{1,4,3,0,2:T(8,128)} fusion(bf16[12,197,3,12,64]{1,4,3,2,0:T(8,128)(2,1)} %bitcast.389, bf16[12,12,197,197]{2,3,1,0:T(8,128)(2,1)} %add_convert_fusion), kind=kOutput, calls=%fused_computation.44 | convolution fusion | flops 726504448 | bytes 26726400 | tf_op jit(solution)/shard_map/transpose(jvp(gqhc,gkhc->ghqk))/dot_general | solution.py:160
  472.5 11.1 %fusion.9 = f32[12,197,1,12,64]{1,4,3,0,2:T(8,128)} fusion(bf16[12,197,3,12,64]{1,4,3,2,0:T(8,128)(2,1)} %bitcast.390, bf16[12,12,197,197]{2,3,1,0:T(8,128)(2,1)} %add_convert_fusion), kind=kOutput, calls=%fused_computation.43 | convolution fusion | flops 726504448 | bytes 26726400 | tf_op jit(solution)/shard_map/transpose(jvp(gqhc,gkhc->ghqk))/dot_general | solution.py:160
  483.6 10.8 %add_convert_fusion.1 = bf16[12,197,3,12,64]{1,4,3,0,2:T(8,128)(2,1)S(1)} fusion(f32[12,197,1,12,64]{1,4,3,0,2:T(8,128)} %fusion.10, f32[12,197,1,12,64]{1,4,3,0,2:T(8,128)} %fusion.9, f32[12,197,1,12,64]{1,4,3,0,2:T(8,128)} %convolution_bitcast_fusion.1), kind=kLoop, calls=%fused_computation.9 | loop fusion | flops 16339968 | bytes 32679936 | tf_op jit(solution)/shard_map/transpose(jvp())/convert_element_type | solution.py:155
  501.6 14.5 %convolution_bitcast_fusion = bf16[768,2304]{1,0:T(8,128)(2,1)} fusion(bf16[12,197,768]{2,1,0:T(8,128)(2,1)} %copy-done.22, bf16[12,197,2304]{1,2,0:T(8,128)(2,1)S(1)} %bitcast.401), kind=kOutput, calls=%fused_computation.33 | convolution fusion | flops 8366063616 | bytes 18063360 | tf_op jit(solution)/shard_map/transpose(jvp(gtd,de->gte))/dot_general | solution.py:155
  516.2 18.1 %fusion.76 = (bf16[768]{0:T(1024)(128)(2,1)S(1)}, f32[12,197]{1,0:T(8,128)S(1)}, f32[12,197,768]{2,1,0:T(8,128)}) fusion(f32[768]{0:T(1024)S(1)} %copy-done.60, f32[12,197,768]{2,1,0:T(8,128)S(1)} %bitcast.384, f32[12,197]{1,0:T(8,128)S(1)} %copy-done.45, bf16[12,197,2304]{1,2,0:T(8,128)(2,1)} %bitcast.402, bf16[768,3200]{1,0:T(8,128)(2,1)S(1)} %bitcast.413), kind=kOutput, calls=%fused_computation.281 | convolution fusion | flops 8375137792 | bytes 29098736 | tf_op jit(solution)/shard_map/transpose(jvp(gtd,de->gte))/dot_general | solution.py:155
  544.3 11.3 %add_convert_fusion.2 = bf16[12,197,768]{2,1,0:T(8,128)(2,1)S(1)} fusion(f32[12,197]{1,0:T(8,128)S(1)} %negate_multiply_fusion.1, f32[12,197]{1,0:T(8,128)S(1)} %copy-done.58, f32[12,197,768]{2,1,0:T(8,128)} %copy-done.6, f32[12,197]{1,0:T(8,128)S(1)} %multiply_multiply_fusion.5, f32[12,197]{1,0:T(8,128)S(1)} %copy-done.45, f32[12,197]{1,0:T(8,128)S(1)} %copy-done.47, ...), kind=kLoop, calls=%fused_computation.24 | loop fusion | flops 21786624 | bytes 32730336 | tf_op jit(solution)/shard_map/convert_element_type | solution.py:246
  568.4 12.2 %collective-permute-done.33 = bf16[4,2,24,1536]{3,2,1,0:T(8,128)(2,1)S(1)} collective-permute-done((bf16[4,2,24,1536]{3,2,1,0:T(8,128)(2,1)S(1)}, bf16[4,2,24,1536]{3,2,1,0:T(8,128)(2,1)S(1)}, u32[]{:S(2)}, u32[]{:S(2)}) %collective-permute-start.33) | collective-permute-done | bytes 589856 | tf_op jit(solution)/shard_map/ppermute | solution.py:36
  (423 shorter events, 238.3 us)
Async XLA Ops:
  3.3 24.0 %collective-permute-start.7 = (bf16[24,1536]{1,0:T(8,128)(2,1)S(1)}, bf16[24,1536]{1,0:T(8,128)(2,1)S(1)}, u32[]{:S(2)}, u32[]{:S(2)}) collective-permute-start(bf16[24,1536]{1,0:T(8,128)(2,1)S(1)} %fusion.66), channel_id=1, source_target_pairs={{0,16},{1,17},{2,18},{3,19},{4,20},{5,21},{6,22},{7,23},{8,24},{9,... | collective-permute-start | bytes 221192 | tf_op jit(solution)/shard_map/ppermute | solution.py:36
  7.4 19.9 %collective-permute-start.6 = (bf16[24,1536]{1,0:T(8,128)(2,1)S(1)}, bf16[24,1536]{1,0:T(8,128)(2,1)S(1)}, u32[]{:S(2)}, u32[]{:S(2)}) collective-permute-start(bf16[24,1536]{1,0:T(8,128)(2,1)S(1)} %fusion.66), channel_id=1, source_target_pairs={{0,8},{1,9},{2,10},{3,11},{4,12},{5,13},{6,14},{7,15},{8,16},{9,17... | collective-permute-start | bytes 221192 | tf_op jit(solution)/shard_map/ppermute | solution.py:36
  9.0 18.4 %collective-permute-start.8 = (bf16[24,1536]{1,0:T(8,128)(2,1)S(1)}, bf16[24,1536]{1,0:T(8,128)(2,1)S(1)}, u32[]{:S(2)}, u32[]{:S(2)}) collective-permute-start(bf16[24,1536]{1,0:T(8,128)(2,1)S(1)} %fusion.66), channel_id=1, source_target_pairs={{0,24},{1,25},{2,26},{3,27},{4,28},{5,29},{6,30},{7,31},{8,0},{9,1... | collective-permute-start | bytes 221192 | tf_op jit(solution)/shard_map/ppermute | solution.py:36
  12.1 16.9 %collective-permute-start.1 = (bf16[24,1664]{1,0:T(8,128)(2,1)S(1)}, bf16[24,1664]{1,0:T(8,128)(2,1)S(1)}, u32[]{:S(2)}, u32[]{:S(2)}) collective-permute-start(bf16[24,1664]{1,0:T(8,128)(2,1)S(1)} %slice.104), channel_id=1, source_target_pairs={{0,16},{1,17},{2,18},{3,19},{4,20},{5,21},{6,22},{7,23},{8,24},{9,... | collective-permute-start | bytes 239624 | tf_op jit(solution)/shard_map/ppermute | solution.py:36
  12.1 16.9 %collective-permute-start.2 = (bf16[24,1664]{1,0:T(8,128)(2,1)S(1)}, bf16[24,1664]{1,0:T(8,128)(2,1)S(1)}, u32[]{:S(2)}, u32[]{:S(2)}) collective-permute-start(bf16[24,1664]{1,0:T(8,128)(2,1)S(1)} %slice.104), channel_id=1, source_target_pairs={{0,24},{1,25},{2,26},{3,27},{4,28},{5,29},{6,30},{7,31},{8,0},{9,1... | collective-permute-start | bytes 239624 | tf_op jit(solution)/shard_map/ppermute | solution.py:36
  27.5 7.8 %collective-permute-start.9 = (bf16[4,24,1536]{2,1,0:T(8,128)(2,1)S(1)}, bf16[4,24,1536]{2,1,0:T(8,128)(2,1)S(1)}, u32[]{:S(2)}, u32[]{:S(2)}) collective-permute-start(bf16[4,24,1536]{2,1,0:T(8,128)(2,1)S(1)} %pad_maximum_fusion.10), channel_id=1, source_target_pairs={{0,2},{1,3},{2,0},{3,1},{4,6},{5,7},{6,4},{7,5},{8,10},{9,11},{10,... | collective-permute-start | bytes 884744 | tf_op jit(solution)/shard_map/ppermute | solution.py:36
  33.7 10.5 %collective-permute-start.3 = (bf16[4,24,1664]{2,1,0:T(8,128)(2,1)S(1)}, bf16[4,24,1664]{2,1,0:T(8,128)(2,1)S(1)}, u32[]{:S(2)}, u32[]{:S(2)}) collective-permute-start(bf16[4,24,1664]{2,1,0:T(8,128)(2,1)S(1)} %pad_maximum_fusion.9), channel_id=1, source_target_pairs={{0,4},{1,5},{2,6},{3,7},{4,0},{5,1},{6,2},{7,3},{8,12},{9,13},{10,... | collective-permute-start | bytes 958472 | tf_op jit(solution)/shard_map/ppermute | solution.py:36
  35.4 17.7 %collective-permute-start.10 = (bf16[2,4,24,1536]{3,2,1,0:T(8,128)(2,1)S(1)}, bf16[2,4,24,1536]{3,2,1,0:T(8,128)(2,1)S(1)}, u32[]{:S(2)}, u32[]{:S(2)}) collective-permute-start(bf16[2,4,24,1536]{3,2,1,0:T(8,128)(2,1)S(1)} %pad_maximum_fusion.8), channel_id=1, source_target_pairs={{0,4},{1,5},{2,6},{3,7},{4,0},{5,1},{6,2},{7,3},{8,12},{9,13},{10,... | collective-permute-start | bytes 1769480 | tf_op jit(solution)/shard_map/ppermute | solution.py:36
  44.4 10.5 %collective-permute-start.4 = (bf16[2,4,24,1664]{3,2,1,0:T(8,128)(2,1)S(1)}, bf16[2,4,24,1664]{3,2,1,0:T(8,128)(2,1)S(1)}, u32[]{:S(2)}, u32[]{:S(2)}) collective-permute-start(bf16[2,4,24,1664]{3,2,1,0:T(8,128)(2,1)S(1)} %pad_maximum_fusion.7), channel_id=1, source_target_pairs={{0,2},{1,3},{2,0},{3,1},{4,6},{5,7},{6,4},{7,5},{8,10},{9,11},{10,... | collective-permute-start | bytes 1916936 | tf_op jit(solution)/shard_map/ppermute | solution.py:36
  54.4 14.5 %collective-permute-start.11 = (bf16[2,2,4,24,1536]{4,3,2,1,0:T(8,128)(2,1)}, bf16[2,2,4,24,1536]{4,3,2,1,0:T(8,128)(2,1)}, u32[]{:S(2)}, u32[]{:S(2)}) collective-permute-start(bf16[2,2,4,24,1536]{4,3,2,1,0:T(8,128)(2,1)} %pad_maximum_fusion.4), channel_id=1, source_target_pairs={{0,1},{1,0},{2,3},{3,2},{4,5},{5,4},{6,7},{7,6},{8,9},{9,8},{10,11... | collective-permute-start | bytes 3538952 | tf_op jit(solution)/shard_map/ppermute | solution.py:36
  56.2 14.2 %collective-permute-start.5 = (bf16[2,2,4,24,1664]{4,3,2,1,0:T(8,128)(2,1)}, bf16[2,2,4,24,1664]{4,3,2,1,0:T(8,128)(2,1)}, u32[]{:S(2)}, u32[]{:S(2)}) collective-permute-start(bf16[2,2,4,24,1664]{4,3,2,1,0:T(8,128)(2,1)} %pad_maximum_fusion.3), channel_id=1, source_target_pairs={{0,1},{1,0},{2,3},{3,2},{4,5},{5,4},{6,7},{7,6},{8,9},{9,8},{10,11... | collective-permute-start | bytes 3833864 | tf_op jit(solution)/shard_map/ppermute | solution.py:36
  188.6 17.3 %collective-permute-start.15 = (bf16[4,16,1536]{2,1,0:T(8,128)(2,1)S(1)}, bf16[4,16,1536]{2,1,0:T(8,128)(2,1)S(1)}, u32[]{:S(2)}, u32[]{:S(2)}) collective-permute-start(bf16[4,16,1536]{2,1,0:T(8,128)(2,1)S(1)} %slice.143), channel_id=1, source_target_pairs={{0,16},{1,17},{2,18},{3,19},{4,20},{5,21},{6,22},{7,23},{8,24},{9,... | collective-permute-start | bytes 589832 | tf_op jit(solution)/shard_map/ppermute | solution.py:36
  188.7 17.3 %collective-permute-start.16 = (bf16[4,16,1536]{2,1,0:T(8,128)(2,1)S(1)}, bf16[4,16,1536]{2,1,0:T(8,128)(2,1)S(1)}, u32[]{:S(2)}, u32[]{:S(2)}) collective-permute-start(bf16[4,16,1536]{2,1,0:T(8,128)(2,1)S(1)} %slice.143), channel_id=1, source_target_pairs={{0,24},{1,25},{2,26},{3,27},{4,28},{5,29},{6,30},{7,31},{8,0},{9,1... | collective-permute-start | bytes 589832 | tf_op jit(solution)/shard_map/ppermute | solution.py:36
  189.1 16.9 %collective-permute-start.14 = (bf16[4,16,1536]{2,1,0:T(8,128)(2,1)S(1)}, bf16[4,16,1536]{2,1,0:T(8,128)(2,1)S(1)}, u32[]{:S(2)}, u32[]{:S(2)}) collective-permute-start(bf16[4,16,1536]{2,1,0:T(8,128)(2,1)S(1)} %slice.143), channel_id=1, source_target_pairs={{0,8},{1,9},{2,10},{3,11},{4,12},{5,13},{6,14},{7,15},{8,16},{9,17... | collective-permute-start | bytes 589832 | tf_op jit(solution)/shard_map/ppermute | solution.py:36
  191.4 27.9 %collective-permute-start.20 = (bf16[2,4,8,1536]{3,2,1,0:T(8,128)(2,1)S(1)}, bf16[2,4,8,1536]{3,2,1,0:T(8,128)(2,1)S(1)}, u32[]{:S(2)}, u32[]{:S(2)}) collective-permute-start(bf16[2,4,8,1536]{3,2,1,0:T(8,128)(2,1)S(1)} %pad_maximum_fusion.14), channel_id=1, source_target_pairs={{0,16},{1,17},{2,18},{3,19},{4,20},{5,21},{6,22},{7,23},{8,24},{9,... | collective-permute-start | bytes 589832 | tf_op jit(solution)/shard_map/ppermute | solution.py:36
  193.8 25.5 %collective-permute-start.21 = (bf16[2,4,8,1536]{3,2,1,0:T(8,128)(2,1)S(1)}, bf16[2,4,8,1536]{3,2,1,0:T(8,128)(2,1)S(1)}, u32[]{:S(2)}, u32[]{:S(2)}) collective-permute-start(bf16[2,4,8,1536]{3,2,1,0:T(8,128)(2,1)S(1)} %pad_maximum_fusion.14), channel_id=1, source_target_pairs={{0,24},{1,25},{2,26},{3,27},{4,28},{5,29},{6,30},{7,31},{8,0},{9,1... | collective-permute-start | bytes 589832 | tf_op jit(solution)/shard_map/ppermute | solution.py:36
  205.9 13.3 %collective-permute-start.19 = (bf16[2,4,8,1536]{3,2,1,0:T(8,128)(2,1)S(1)}, bf16[2,4,8,1536]{3,2,1,0:T(8,128)(2,1)S(1)}, u32[]{:S(2)}, u32[]{:S(2)}) collective-permute-start(bf16[2,4,8,1536]{3,2,1,0:T(8,128)(2,1)S(1)} %pad_maximum_fusion.14), channel_id=1, source_target_pairs={{0,8},{1,9},{2,10},{3,11},{4,12},{5,13},{6,14},{7,15},{8,16},{9,17... | collective-permute-start | bytes 589832 | tf_op jit(solution)/shard_map/ppermute | solution.py:36
  206.2 15.9 %collective-permute-start.17 = (bf16[4,4,16,1536]{3,2,1,0:T(8,128)(2,1)S(1)}, bf16[4,4,16,1536]{3,2,1,0:T(8,128)(2,1)S(1)}, u32[]{:S(2)}, u32[]{:S(2)}) collective-permute-start(bf16[4,4,16,1536]{3,2,1,0:T(8,128)(2,1)S(1)} %pad_maximum_fusion.5), channel_id=1, source_target_pairs={{0,4},{1,5},{2,6},{3,7},{4,0},{5,1},{6,2},{7,3},{8,12},{9,13},{10,... | collective-permute-start | bytes 2359304 | tf_op jit(solution)/shard_map/ppermute | solution.py:36
  265.8 16.9 %collective-permute-start.26 = (bf16[2,4,8,1536]{3,1,0,2:T(4,128)(2,1)S(1)}, bf16[2,4,8,1536]{3,1,0,2:T(4,128)(2,1)S(1)}, u32[]{:S(2)}, u32[]{:S(2)}) collective-permute-start(bf16[2,4,8,1536]{3,1,0,2:T(4,128)(2,1)S(1)} %get-tuple-element.142), channel_id=1, source_target_pairs={{0,8},{1,9},{2,10},{3,11},{4,12},{5,13},{6,14},{7,15},{8,16},{9,17... | collective-permute-start | bytes 589832 | tf_op jit(solution)/shard_map/ppermute | solution.py:36
  277.3 7.8 %collective-permute-start.28 = (bf16[2,4,8,1536]{3,1,0,2:T(4,128)(2,1)S(1)}, bf16[2,4,8,1536]{3,1,0,2:T(4,128)(2,1)S(1)}, u32[]{:S(2)}, u32[]{:S(2)}) collective-permute-start(bf16[2,4,8,1536]{3,1,0,2:T(4,128)(2,1)S(1)} %get-tuple-element.143), channel_id=1, source_target_pairs={{0,24},{1,25},{2,26},{3,27},{4,28},{5,29},{6,30},{7,31},{8,0},{9,1... | collective-permute-start | bytes 589832 | tf_op jit(solution)/shard_map/ppermute | solution.py:36
  277.3 14.0 %collective-permute-start.27 = (bf16[2,4,8,1536]{3,1,0,2:T(4,128)(2,1)S(1)}, bf16[2,4,8,1536]{3,1,0,2:T(4,128)(2,1)S(1)}, u32[]{:S(2)}, u32[]{:S(2)}) collective-permute-start(bf16[2,4,8,1536]{3,1,0,2:T(4,128)(2,1)S(1)} %get-tuple-element.144), channel_id=1, source_target_pairs={{0,16},{1,17},{2,18},{3,19},{4,20},{5,21},{6,22},{7,23},{8,24},{9,... | collective-permute-start | bytes 589832 | tf_op jit(solution)/shard_map/ppermute | solution.py:36
  281.6 16.8 %collective-permute-start.22 = (bf16[4,4,16,1536]{3,1,0,2:T(4,128)(2,1)S(1)}, bf16[4,4,16,1536]{3,1,0,2:T(4,128)(2,1)S(1)}, u32[]{:S(2)}, u32[]{:S(2)}) collective-permute-start(bf16[4,4,16,1536]{3,1,0,2:T(4,128)(2,1)S(1)} %dynamic-slice_bitcast_fusion.1), channel_id=1, source_target_pairs={{0,4},{1,5},{2,6},{3,7},{4,0},{5,1},{6,2},{7,3},{8,12},{9,13},{10,... | collective-permute-start | bytes 2359304 | tf_op jit(solution)/shard_map/ppermute | solution.py:36
  291.6 11.5 %collective-permute-start.29 = (bf16[4,8,1536]{2,0,1:T(4,128)(2,1)S(1)}, bf16[4,8,1536]{2,0,1:T(4,128)(2,1)S(1)}, u32[]{:S(2)}, u32[]{:S(2)}) collective-permute-start(bf16[4,8,1536]{2,0,1:T(4,128)(2,1)S(1)} %dynamic-slice_bitcast_fusion.12), channel_id=1, source_target_pairs={{0,4},{1,5},{2,6},{3,7},{4,0},{5,1},{6,2},{7,3},{8,12},{9,13},{10,... | collective-permute-start | bytes 294920 | tf_op jit(solution)/shard_map/ppermute | solution.py:36
  299.2 7.6 %collective-permute-start.23 = (bf16[4,16,1536]{2,0,1:T(4,128)(2,1)S(1)}, bf16[4,16,1536]{2,0,1:T(4,128)(2,1)S(1)}, u32[]{:S(2)}, u32[]{:S(2)}) collective-permute-start(bf16[4,16,1536]{2,0,1:T(4,128)(2,1)S(1)} %get-tuple-element.145), channel_id=1, source_target_pairs={{0,8},{1,9},{2,10},{3,11},{4,12},{5,13},{6,14},{7,15},{8,16},{9,17... | collective-permute-start | bytes 589832 | tf_op jit(solution)/shard_map/ppermute | solution.py:36
  299.6 8.7 %collective-permute-start.25 = (bf16[4,16,1536]{2,0,1:T(4,128)(2,1)S(1)}, bf16[4,16,1536]{2,0,1:T(4,128)(2,1)S(1)}, u32[]{:S(2)}, u32[]{:S(2)}) collective-permute-start(bf16[4,16,1536]{2,0,1:T(4,128)(2,1)S(1)} %get-tuple-element.146), channel_id=1, source_target_pairs={{0,24},{1,25},{2,26},{3,27},{4,28},{5,29},{6,30},{7,31},{8,0},{9,1... | collective-permute-start | bytes 589832 | tf_op jit(solution)/shard_map/ppermute | solution.py:36
  303.1 11.5 %collective-permute-start.24 = (bf16[4,16,1536]{2,0,1:T(4,128)(2,1)S(1)}, bf16[4,16,1536]{2,0,1:T(4,128)(2,1)S(1)}, u32[]{:S(2)}, u32[]{:S(2)}) collective-permute-start(bf16[4,16,1536]{2,0,1:T(4,128)(2,1)S(1)} %get-tuple-element.147), channel_id=1, source_target_pairs={{0,16},{1,17},{2,18},{3,19},{4,20},{5,21},{6,22},{7,23},{8,24},{9,... | collective-permute-start | bytes 589832 | tf_op jit(solution)/shard_map/ppermute | solution.py:36
  543.8 20.9 %collective-permute-start.32 = (bf16[4,2,2,24,1536]{4,3,2,1,0:T(8,128)(2,1)S(1)}, bf16[4,2,2,24,1536]{4,3,2,1,0:T(8,128)(2,1)S(1)}, u32[]{:S(2)}, u32[]{:S(2)}) collective-permute-start(bf16[4,2,2,24,1536]{4,3,2,1,0:T(8,128)(2,1)S(1)} %dynamic-slice_bitcast_fusion), channel_id=1, source_target_pairs={{0,1},{1,0},{2,3},{3,2},{4,5},{5,4},{6,7},{7,6},{8,9},{9,8},{10,11... | collective-permute-start | bytes 3538952 | tf_op jit(solution)/shard_map/ppermute | solution.py:36
  556.2 10.2 %collective-permute-start.38 = (bf16[4,2,2,24,1664]{4,3,0,1,2:T(8,128)(2,1)S(1)}, bf16[4,2,2,24,1664]{4,3,0,1,2:T(8,128)(2,1)S(1)}, u32[]{:S(2)}, u32[]{:S(2)}) collective-permute-start(bf16[4,2,2,24,1664]{4,3,0,1,2:T(8,128)(2,1)S(1)} %bitcast.424), channel_id=1, source_target_pairs={{0,1},{1,0},{2,3},{3,2},{4,5},{5,4},{6,7},{7,6},{8,9},{9,8},{10,11... | collective-permute-start | bytes 3833864 | tf_op jit(solution)/shard_map/ppermute | solution.py:36
  565.1 15.5 %collective-permute-start.33 = (bf16[4,2,24,1536]{3,2,1,0:T(8,128)(2,1)S(1)}, bf16[4,2,24,1536]{3,2,1,0:T(8,128)(2,1)S(1)}, u32[]{:S(2)}, u32[]{:S(2)}) collective-permute-start(bf16[4,2,24,1536]{3,2,1,0:T(8,128)(2,1)S(1)} %dynamic-slice_bitcast_fusion.3), channel_id=1, source_target_pairs={{0,4},{1,5},{2,6},{3,7},{4,0},{5,1},{6,2},{7,3},{8,12},{9,13},{10,... | collective-permute-start | bytes 1769480 | tf_op jit(solution)/shard_map/ppermute | solution.py:36
  566.8 16.5 %collective-permute-start.39 = (bf16[4,2,24,1664]{3,2,0,1:T(8,128)(2,1)S(1)}, bf16[4,2,24,1664]{3,2,0,1:T(8,128)(2,1)S(1)}, u32[]{:S(2)}, u32[]{:S(2)}) collective-permute-start(bf16[4,2,24,1664]{3,2,0,1:T(8,128)(2,1)S(1)} %dynamic-slice_bitcast_fusion.2), channel_id=1, source_target_pairs={{0,2},{1,3},{2,0},{3,1},{4,6},{5,7},{6,4},{7,5},{8,10},{9,11},{10,... | collective-permute-start | bytes 1916936 | tf_op jit(solution)/shard_map/ppermute | solution.py:36
  580.7 8.6 %collective-permute-start.34 = (bf16[4,24,1536]{2,1,0:T(8,128)(2,1)S(1)}, bf16[4,24,1536]{2,1,0:T(8,128)(2,1)S(1)}, u32[]{:S(2)}, u32[]{:S(2)}) collective-permute-start(bf16[4,24,1536]{2,1,0:T(8,128)(2,1)S(1)} %dynamic-slice_bitcast_fusion.5), channel_id=1, source_target_pairs={{0,2},{1,3},{2,0},{3,1},{4,6},{5,7},{6,4},{7,5},{8,10},{9,11},{10,... | collective-permute-start | bytes 884744 | tf_op jit(solution)/shard_map/ppermute | solution.py:36
  593.4 7.7 %collective-permute-start.40 = (bf16[4,24,1664]{2,1,0:T(8,128)(2,1)S(1)}, bf16[4,24,1664]{2,1,0:T(8,128)(2,1)S(1)}, u32[]{:S(2)}, u32[]{:S(2)}) collective-permute-start(bf16[4,24,1664]{2,1,0:T(8,128)(2,1)S(1)} %dynamic-slice_bitcast_fusion.4), channel_id=1, source_target_pairs={{0,4},{1,5},{2,6},{3,7},{4,0},{5,1},{6,2},{7,3},{8,12},{9,13},{10,... | collective-permute-start | bytes 958472 | tf_op jit(solution)/shard_map/ppermute | solution.py:36
  (99 other events, 1212.4 us)

commit v2 on v1

v2 whole, which is shorter than its diff:
```python
from functools import partial

import jax
import jax.numpy as jnp
from jax import lax
from jax.experimental import pallas as pl
from jax.experimental.pallas import tpu as pltpu
from jax.sharding import PartitionSpec as P

HEADS = 12
HEAD_DIM = 64
EPSILON = 1e-06
BOTH = ("dp", "expert")
F32, BF16 = jnp.float32, jnp.bfloat16
LOW = -1e30
VMEM_LIMIT = 60 * 1024 * 1024
CHUNKS = 1


class Grid:
    def __init__(self, n, m):
        self.n, self.m = n, m
        self.size = {"z": n // 2, "y": 2, "x": m // 2, "c": 2}

    def coords(self):
        d, e = lax.axis_index("dp"), lax.axis_index("expert")
        return {"z": d // 2, "y": d % 2, "x": e // 2, "c": e % 2}

    def perm(self, axis, k):
        pairs = []
        for z in range(self.size["z"]):
            for y in range(2):
                for x in range(self.size["x"]):
                    for c in range(2):
                        p = {"z": z, "y": y, "x": x, "c": c}
                        q = dict(p)
                        q[axis] = (q[axis] + k) % self.size[axis]
                        pairs.append(tuple((r["z"] * 2 + r["y"]) * self.m + r["x"] * 2 + r["c"] for r in (p, q)))
        return pairs

    def send(self, a, axis, k):
        return lax.ppermute(a, BOTH, self.perm(axis, k))

    def by_coordinate(self, me, axis, pieces):
        s = self.size[axis]
        if s == 2:
            return jnp.stack([jnp.where(me == p, pieces[0], pieces[1]) for p in range(2)])
        if s <= 4:
            return jnp.stack([lax.select_n((me - p) % s, *pieces) for p in range(s)])
        out = jnp.zeros((s,) + pieces[0].shape, pieces[0].dtype)
        for k in range(s):
            out = lax.dynamic_update_index_in_dim(out, pieces[k], (me - k) % s, 0)
        return out

    def gather(self, a, axis, me):
        pieces = [a] + [self.send(a, axis, k) for k in range(1, self.size[axis])]
        return self.by_coordinate(me[axis], axis, pieces)

    def block(self, a, axis, me, k):
        return lax.dynamic_index_in_dim(a, (me[axis] + k) % self.size[axis], 0, keepdims=False)

    def scatter_sum(self, a, axis, me):
        own = self.block(a, axis, me, 0).astype(jnp.float32)
        for k in range(1, self.size[axis]):
            own = own + self.send(self.block(a, axis, me, k), axis, k).astype(jnp.float32)
        return own

    def exchange(self, a, axis, me):
        pieces = [self.block(a, axis, me, k) for k in range(self.size[axis])]
        pieces = pieces[:1] + [self.send(p, axis, k) for k, p in enumerate(pieces) if k]
        return self.by_coordinate(me[axis], axis, pieces)


def joined(parts, axis):
    return jnp.concatenate(parts, axis=axis) if len(parts) > 1 else parts[0]


def gather_rows(grid, a, cuts, me):
    outs, low = [], 0
    for width, order in cuts:
        b, done = a[:, low : low + width], []
        low += width
        for axis in order:
            b = grid.gather(b, axis, me)
            done.insert(0, axis)
        outs.append(jnp.transpose(b, [done.index(axis) for axis in "zyxc"] + [4, 5]))
    return joined(outs, -1).reshape(-1, a.shape[1])


def reduce_rows(grid, a, cuts, me):
    s = grid.size
    a = a.reshape(s["z"], 2, s["x"], 2, -1, a.shape[1])
    outs, low = [], 0
    for width, order in cuts:
        b, left = a[..., low : low + width], ["z", "y", "x", "c"]
        low += width
        for axis in order:
            b = jnp.moveaxis(b.astype(jnp.bfloat16), left.index(axis), 0)
            b = grid.scatter_sum(b, axis, me)
            left.remove(axis)
        outs.append(b)
    return joined(outs, -1)


def to_experts(grid, a, part, me):
    s = grid.size
    b = grid.exchange(a.reshape(s["x"], 2, *a.shape[1:]), "x", me)
    b = grid.exchange(jnp.moveaxis(b, 1, 0), "c", me)
    b = jnp.moveaxis(b, 0, 1).reshape(a.shape)
    first = grid.gather(grid.gather(b[:, :part], "z", me), "y", me)
    second = grid.gather(grid.gather(b[:, part:], "y", me), "z", me)
    r = jnp.concatenate([jnp.moveaxis(first, 0, 1), second], axis=3)
    return r.reshape(grid.n, *a.shape)


def from_experts(grid, a, part, me):
    s = grid.size
    b = a.reshape(s["z"], 2, *a.shape[1:])
    first = grid.scatter_sum(jnp.moveaxis(b[:, :, :, :part], 1, 0), "y", me).astype(jnp.bfloat16)
    first = grid.scatter_sum(first, "z", me)
    second = grid.scatter_sum(b[:, :, :, part:], "z", me).astype(jnp.bfloat16)
    second = grid.scatter_sum(second, "y", me)
    r = jnp.concatenate([first, second], axis=1).astype(jnp.bfloat16)
    r = grid.exchange(r.reshape(s["x"], 2, *r.shape[1:]), "x", me)
    r = grid.exchange(jnp.moveaxis(r, 1, 0), "c", me)
    return jnp.moveaxis(r, 0, 1).reshape(a.shape[1:])


def dot(a, b, ca=1, cb=0):
    return lax.dot_general(a, b, (((ca,), (cb,)), ((), ())), preferred_element_type=F32)


def standardized(v):
    width = v.shape[-1]
    center = v - jnp.sum(v, axis=-1, keepdims=True) * (1.0 / width)
    root = lax.rsqrt(jnp.sum(center * center, axis=-1, keepdims=True) * (1.0 / width) + EPSILON)
    return center * root, root


def head_masks():
    lane = lax.broadcasted_iota(jnp.int32, (1, 2 * HEAD_DIM), 1)
    return [(lane // HEAD_DIM == h) for h in range(2)]


def routed(logits, tokens, slots):
    row = lax.broadcasted_iota(jnp.int32, logits.shape, 0)
    lane = lax.broadcasted_iota(jnp.int32, logits.shape, 1)
    valid = (row < tokens) & (lane < slots)
    kept = jnp.where(valid, logits, LOW)
    down = jnp.where(valid, jnp.exp(kept - jnp.max(kept, axis=0, keepdims=True)), 0.0)
    down_sum = jnp.sum(down, axis=0, keepdims=True)
    over_tokens = down * (1.0 / jnp.where(down_sum > 0, down_sum, 1.0))
    across = jnp.where(valid, jnp.exp(kept - jnp.max(kept, axis=1, keepdims=True)), 0.0)
    across_sum = jnp.sum(across, axis=1, keepdims=True)
    over_slots = across * (1.0 / jnp.where(across_sum > 0, across_sum, 1.0))
    return over_tokens, over_slots


def forward_kernel(tokens, slots, live, x_ref, cot_ref, wqkv_ref, wout_ref, phi_ref, vec_ref,
                   n1_ref, triple_ref, mixed_ref, hidden_ref, logits_ref, slot_ref, grad_slot_ref, pad_ref):
    i = pl.program_id(0)
    rows, features = pad_ref.shape
    keys = triple_ref.shape[1]

    @pl.when(i == 0)
    def _():
        pad_ref[...] = jnp.zeros_like(pad_ref)

    @pl.when(live[i] == 0)
    def _():
        n1_ref[...] = jnp.zeros_like(n1_ref)
        mixed_ref[...] = jnp.zeros_like(mixed_ref)
        slot_ref[...] = jnp.zeros_like(slot_ref)
        grad_slot_ref[...] = jnp.zeros_like(grad_slot_ref)

    @pl.when(live[i] != 0)
    def _():
        pad_ref[:tokens] = x_ref[0, 0].astype(F32)
        x = pad_ref[...]
        n1, _ = standardized(x)
        n1_ref[0] = n1.astype(BF16)
        normed = (n1 * vec_ref[0:1] + vec_ref[1:2]).astype(BF16)
        for part in range(3):
            cut = slice(part * features, (part + 1) * features)
            triple_ref[0, :rows, cut] = dot(normed, wqkv_ref[:, cut]).astype(BF16)
        triple_ref[0, rows:, :] = jnp.zeros((keys - rows, 3 * features), BF16)
        bias = jnp.where(lax.broadcasted_iota(jnp.int32, (1, keys), 1) < tokens, 0.0, LOW)
        masks = head_masks()
        for pair in range(HEADS // 2):
            low = pair * 2 * HEAD_DIM
            q = triple_ref[0, :rows, low:low + 128]
            k = triple_ref[0, :, features + low:features + low + 128]
            v = triple_ref[0, :, 2 * features + low:2 * features + low + 128]
            total = None
            for mask in masks:
                scale = jnp.where(mask, HEAD_DIM ** -0.5, 0.0).astype(BF16)
                scores = dot(q * scale, k, 1, 1) + bias
                powers = jnp.exp(scores - jnp.max(scores, axis=1, keepdims=True))
                attention = (powers * (1.0 / jnp.sum(powers, axis=1, keepdims=True))).astype(BF16)
                part = dot(attention, v * jnp.where(mask, 1.0, 0.0).astype(BF16))
                total = part if total is None else total + part
            mixed_ref[0, :, low:low + 128] = total.astype(BF16)
        hidden = pad_ref[...] + dot(mixed_ref[0], wout_ref[...])
        hidden_ref[0] = hidden
        n2, _ = standardized(hidden)
        normed_two = (n2 * vec_ref[2:3] + vec_ref[3:4]).astype(BF16)
        logits = dot(normed_two, phi_ref[...])
        logits_ref[0] = logits
        dispatch, combine = routed(logits, tokens, slots)
        kept = slot_ref.shape[1]
        slot_ref[0] = dot(dispatch.astype(BF16), normed_two, 0, 0)[:kept].astype(BF16)
        pad_ref[:tokens] = cot_ref[0, 0].astype(F32)
        grad_slot_ref[0] = dot(combine.astype(BF16), pad_ref[...].astype(BF16), 0, 0)[:kept].astype(BF16)


def backward_kernel(tokens, slots, live, cot_ref, triple_ref, hidden_ref, logits_ref, slot_out_ref, grad_in_ref,
                    woutt_ref, phit_ref, vec_ref,
                    out_ref, grad_branch_ref, grad_triple_ref, small_ref, pad_ref, gm_ref):
    i = pl.program_id(0)
    rows, features = pad_ref.shape
    keys = triple_ref.shape[1]

    @pl.when(i == 0)
    def _():
        pad_ref[...] = jnp.zeros_like(pad_ref)
        gm_ref[...] = jnp.zeros_like(gm_ref)
        small_ref[...] = jnp.zeros_like(small_ref)

    @pl.when(live[i] == 0)
    def _():
        out_ref[...] = jnp.zeros_like(out_ref)
        grad_branch_ref[...] = jnp.zeros_like(grad_branch_ref)
        grad_triple_ref[...] = jnp.zeros_like(grad_triple_ref)

    @pl.when(live[i] != 0)
    def _():
        hidden = hidden_ref[0]
        n2, root = standardized(hidden)
        gain = vec_ref[2:3]
        normed_two = (n2 * gain + vec_ref[3:4]).astype(BF16)
        over_tokens, over_slots = routed(logits_ref[0], tokens, slots)
        dispatch, combine = over_tokens.astype(BF16), over_slots.astype(BF16)
        slot_out, grad_in = slot_out_ref[0], grad_in_ref[0]
        pad_ref[:tokens] = cot_ref[0, 0].astype(F32)
        cot = pad_ref[...]
        result = hidden + dot(combine, slot_out)
        out_ref[0, 0] = result[:tokens].astype(BF16)
        grad_combine = dot(cot.astype(BF16), slot_out, 1, 1)
        grad_dispatch = dot(normed_two, grad_in, 1, 1)
        grad_logits = over_tokens * (grad_dispatch - jnp.sum(grad_dispatch * over_tokens, axis=0, keepdims=True))
        grad_logits += over_slots * (grad_combine - jnp.sum(grad_combine * over_slots, axis=1, keepdims=True))
        grad_logits = grad_logits.astype(BF16)
        grad_two = dot(dispatch, grad_in) + dot(grad_logits, phit_ref[...])
        small_ref[0:1] += jnp.sum(grad_two * n2, axis=0, keepdims=True)
        small_ref[1:2] += jnp.sum(grad_two, axis=0, keepdims=True)
        kept = small_ref.shape[0] - 8
        small_ref[8:] += dot(grad_logits, normed_two, 0, 0)[:kept]
        u = grad_two * gain
        inner = u - jnp.sum(u, axis=-1, keepdims=True) * (1.0 / features)
        inner = inner - n2 * (jnp.sum(u * n2, axis=-1, keepdims=True) * (1.0 / features))
        grad_branch = (cot + root * inner).astype(BF16)
        grad_branch_ref[0] = grad_branch
        gm_ref[:rows] = dot(grad_branch, woutt_ref[...]).astype(BF16)
        valid = lax.broadcasted_iota(jnp.int32, (rows, 1), 0) < tokens
        for pair in range(HEADS // 2):
            low = pair * 2 * HEAD_DIM
            q = triple_ref[0, :, low:low + 128]
            k = triple_ref[0, :rows, features + low:features + low + 128]
            v = triple_ref[0, :rows, 2 * features + low:2 * features + low + 128]
            gm = gm_ref[:, low:low + 128]
            grad_q = grad_k = grad_v = None
            for mask in head_masks():
                one = jnp.where(mask, 1.0, 0.0).astype(BF16)
                scale = jnp.where(mask, HEAD_DIM ** -0.5, 0.0).astype(BF16)
                q_own, gm_own = q * scale, gm * one
                scores = jnp.where(valid, dot(k, q_own, 1, 1), LOW)
                powers = jnp.exp(scores - jnp.max(scores, axis=0, keepdims=True))
                attention = powers * (1.0 / jnp.sum(powers, axis=0, keepdims=True))
                grad_attention = dot(v, gm_own, 1, 1)
                mean = jnp.sum(grad_attention * attention, axis=0, keepdims=True)
                grad_scores = (attention * (grad_attention - mean)).astype(BF16)
                parts = (dot(grad_scores, k * scale, 0, 0), dot(grad_scores, q_own), dot(attention.astype(BF16), gm_own))
                if grad_q is None:
                    grad_q, grad_k, grad_v = parts
                else:
                    grad_q, grad_k, grad_v = grad_q + parts[0], grad_k + parts[1], grad_v + parts[2]
            grad_triple_ref[0, :, low:low + 128] = grad_q[:rows].astype(BF16)
            grad_triple_ref[0, :, features + low:features + low + 128] = grad_k.astype(BF16)
            grad_triple_ref[0, :, 2 * features + low:2 * features + low + 128] = grad_v.astype(BF16)


def input_kernel(tokens, live, x_ref, grad_triple_ref, grad_branch_ref, wqkvt_ref, vec_ref, out_ref, pad_ref):
    i = pl.program_id(0)
    features = pad_ref.shape[1]

    @pl.when(i == 0)
    def _():
        pad_ref[...] = jnp.zeros_like(pad_ref)

    @pl.when(live[i] == 0)
    def _():
        out_ref[...] = jnp.zeros_like(out_ref)

    @pl.when(live[i] != 0)
    def _():
        pad_ref[:tokens] = x_ref[0, 0].astype(F32)
        n1, root = standardized(pad_ref[...])
        v = dot(grad_triple_ref[0], wqkvt_ref[...]) * vec_ref[0:1]
        inner = v - jnp.sum(v, axis=-1, keepdims=True) * (1.0 / features)
        inner = inner - n1 * (jnp.sum(v * n1, axis=-1, keepdims=True) * (1.0 / features))
        grad = grad_branch_ref[0].astype(F32) + root * inner
        out_ref[0, 0] = grad[:tokens].astype(BF16)


def image_spec(tokens, features, capacity, first):
    return pl.BlockSpec((1, 1, tokens, features), lambda i, live: ((i + first) // capacity, (i + first) % capacity, 0, 0))


def own(*shape):
    return pl.BlockSpec((1,) + shape, lambda i, live: (i,) + (0,) * len(shape))


def fixed(*shape):
    return pl.BlockSpec(shape, lambda i, live: (0,) * len(shape), pipeline_mode=pl.Buffered(1))


def call(kernel, images, in_specs, out_specs, out_shape, scratch):
    return pl.pallas_call(
        kernel,
        grid_spec=pltpu.PrefetchScalarGridSpec(num_scalar_prefetch=1, grid=(images,), in_specs=in_specs, out_specs=out_specs, scratch_shapes=scratch),
        out_shape=out_shape,
        compiler_params=pltpu.CompilerParams(vmem_limit_bytes=VMEM_LIMIT, dimension_semantics=("arbitrary",)),
    )


def padded(v, step):
    return -(-v // step) * step


def forward(live, inputs, cotangent, wqkv, wout, phi, vectors, slots, first, images):
    capacity, tokens, features = inputs.shape[1:]
    rows, keys, kept = padded(tokens, 16), padded(tokens, 128), padded(slots, 16)
    image = image_spec(tokens, features, capacity, first)
    shape = jax.ShapeDtypeStruct
    return call(
        partial(forward_kernel, tokens, slots), images,
        [image, image, fixed(*wqkv.shape), fixed(*wout.shape), fixed(*phi.shape), fixed(*vectors.shape)],
        [own(rows, features), own(keys, 3 * features), own(rows, features), own(rows, features), own(rows, 128), own(kept, features), own(kept, features)],
        [shape((images, rows, features), BF16), shape((images, keys, 3 * features), BF16), shape((images, rows, features), BF16),
         shape((images, rows, features), F32), shape((images, rows, 128), F32), shape((images, kept, features), BF16), shape((images, kept, features), BF16)],
        [pltpu.VMEM((rows, features), F32)],
    )(live, inputs, cotangent, wqkv, wout, phi, vectors)


def backward(live, cotangent, triple, hidden, logits, slot_out, grad_in, woutt, phit, vectors, slots, first):
    capacity, tokens, features = cotangent.shape[1:]
    images, rows = hidden.shape[:2]
    keys, kept = triple.shape[1], padded(slots, 8)
    image = image_spec(tokens, features, capacity, first)
    shape = jax.ShapeDtypeStruct
    return call(
        partial(backward_kernel, tokens, slots), images,
        [image, own(keys, 3 * features), own(rows, features), own(rows, 128), own(128, features), own(128, features),
         fixed(*woutt.shape), fixed(*phit.shape), fixed(*vectors.shape)],
        [pl.BlockSpec((1, 1, tokens, features), lambda i, live: (i, 0, 0, 0)), own(rows, features), own(rows, 3 * features), pl.BlockSpec((8 + kept, features), lambda i, live: (0, 0))],
        [shape((images, 1, tokens, features), BF16), shape((images, rows, features), BF16), shape((images, rows, 3 * features), BF16), shape((8 + kept, features), F32)],
        [pltpu.VMEM((rows, features), F32), pltpu.VMEM((keys, features), BF16)],
    )(live, cotangent, triple, hidden, logits, slot_out, grad_in, woutt, phit, vectors)


def input_backward(live, inputs, grad_triple, grad_branch, wqkvt, vectors, first):
    capacity, tokens, features = inputs.shape[1:]
    images, rows = grad_branch.shape[:2]
    shape = jax.ShapeDtypeStruct
    return call(
        partial(input_kernel, tokens), images,
        [image_spec(tokens, features, capacity, first), own(rows, 3 * features), own(rows, features), fixed(*wqkvt.shape), fixed(*vectors.shape)],
        [pl.BlockSpec((1, 1, tokens, features), lambda i, live: (i, 0, 0, 0))],
        [shape((images, 1, tokens, features), BF16)],
        [pltpu.VMEM((rows, features), F32)],
    )(live, inputs, grad_triple, grad_branch, wqkvt, vectors)[0]


def experts(rows, grads, up, down):
    pre = jnp.einsum("srd,sdf->srf", rows, up, preferred_element_type=F32)
    active, slope = jax.vjp(partial(jax.nn.gelu, approximate=False), pre)
    active = active.astype(BF16)
    out = jnp.einsum("srf,sfd->srd", active, down, preferred_element_type=F32)
    grad_active = jnp.einsum("srd,sfd->srf", grads, down, preferred_element_type=F32)
    grad_pre = slope(grad_active)[0].astype(BF16)
    grad_rows = jnp.einsum("srf,sdf->srd", grad_pre, up, preferred_element_type=F32)
    return (out, grad_rows, active, grad_pre)


def columns(vectors, table):
    small = jnp.concatenate([jnp.stack(vectors, axis=1), table], axis=1)
    return jnp.pad(small, ((0, 0), (0, 128 - small.shape[1])))


def body(grid, inputs, counts, ln1_gain, ln1_bias, w_qkv, w_out, ln2_gain, ln2_bias, phi, w_up, w_down, cotangent):
    me = grid.coords()
    batches, capacity, tokens, features = inputs.shape
    slots = phi.shape[1]
    per = slots // grid.m
    packed = jnp.concatenate([w_qkv, w_out, columns([ln1_gain, ln1_bias, ln2_gain, ln2_bias], phi)], axis=1)
    whole = gather_rows(grid, packed, ((1664, "zyxc"), (1536, "zxyc")), me)
    wqkv, wout, small = whole[:, : 3 * features], whole[:, 3 * features : 4 * features], whole[:, 4 * features :]
    vectors = jnp.pad(small[:, :4].T.astype(F32), ((0, 4), (0, 0)))
    phi_all = jnp.pad(small[:, 4 : 4 + slots], ((0, 0), (0, 128 - slots)))
    live = (jnp.arange(capacity)[None, :] < counts).astype(jnp.int32).reshape(-1)

    chunks = []
    step = batches * capacity // CHUNKS
    for c in range(CHUNKS):
        own_live = live[c * step : (c + 1) * step]
        kept = forward(own_live, inputs, cotangent, wqkv, wout, phi_all, vectors, slots, c * step, step)
        leaving = jnp.stack([kept[5][:, :slots], kept[6][:, :slots]]).reshape(2, step, grid.m, per, features)
        leaving = leaving.transpose(2, 3, 0, 1, 4).reshape(grid.m, per * 2 * step, features)
        chunks.append([own_live, kept, leaving])
    part = padded(per * 2 * step * 2 // 3, 8)
    for c in range(CHUNKS):
        arrived = to_experts(grid, chunks[c][2], part, me)
        arrived = arrived.reshape(grid.n * grid.m, per, 2, step, features)
        rows, grads = (arrived[:, :, k].transpose(1, 0, 2, 3).reshape(per, -1, features) for k in range(2))
        out, grad_rows, active, grad_pre = experts(rows, grads, w_up, w_down)
        back = jnp.stack([a.astype(BF16).reshape(per, grid.n, grid.m, step, features) for a in (out, grad_rows)])
        back = back.transpose(2, 3, 1, 0, 4, 5).reshape(grid.n, grid.m, per * 2 * step, features)
        home = from_experts(grid, back, part, me).reshape(grid.m, per, 2, step, features)
        home = home.transpose(2, 3, 0, 1, 4).reshape(2, step, slots, features)
        chunks[c] += [(rows, grads, active, grad_pre), jnp.pad(home, ((0, 0), (0, 0), (0, 128 - slots), (0, 0)))]
    outs, grads_out, small, made = [], [], 0.0, []
    for c, (own_live, kept, _, _, home) in enumerate(chunks):
        out, grad_branch, grad_triple, sums = backward(
            own_live, cotangent, kept[1], kept[3], kept[4], home[0], home[1], wout.T, phi_all.T, vectors, slots, c * step
        )
        outs.append(out)
        small = small + sums
        made.append((kept[0], kept[2], grad_branch, grad_triple))
    rows, grads, active, grad_pre = (joined([c[3][k] for c in chunks], 1) for k in range(4))
    grad_up = jnp.einsum("srd,srf->sdf", rows, grad_pre, preferred_element_type=F32)
    grad_down = jnp.einsum("srf,srd->sfd", active, grads, preferred_element_type=F32)
    n1, mixed, grad_branch, grad_triple = (joined([m[k] for m in made], 0).reshape(-1, made[0][k].shape[-1]) for k in range(4))
    product = dot(n1, grad_triple, 0, 0)
    total = jnp.sum(grad_triple.astype(F32), axis=0, keepdims=True)
    grad_wqkv = vectors[0][:, None] * product + vectors[1][:, None] * total
    grad_ln1_gain = jnp.sum(wqkv.astype(F32) * product, axis=1)
    grad_ln1_bias = jnp.sum(wqkv.astype(F32) * total, axis=1)
    grad_wout = dot(mixed, grad_branch, 0, 0)
    small = columns([grad_ln1_gain, grad_ln1_bias, small[0], small[1]], small[8 : 8 + slots].T)
    packed = jnp.concatenate([grad_wqkv.astype(BF16), grad_wout.astype(BF16), small.astype(BF16)], axis=1)
    sums = reduce_rows(grid, packed, ((1664, "cxyz"), (1536, "cyxz")), me)
    small = sums[:, 4 * features :]
    for c, (own_live, _, _, _, _) in enumerate(chunks):
        grads_out.append(input_backward(own_live, inputs, made[c][3], made[c][2], wqkv.T, vectors, c * step))
    return (
        joined(outs, 0).reshape(inputs.shape),
        joined(grads_out, 0).reshape(inputs.shape),
        small[:, 0],
        small[:, 1],
        sums[:, : 3 * features],
        sums[:, 3 * features : 4 * features],
        small[:, 2],
        small[:, 3],
        small[:, 4 : 4 + slots],
        grad_up,
        grad_down,
    )


def solution(mesh):
    rows = P(BOTH, None)
    row = P(BOTH)
    image = P(None, BOTH, None, None)
    up, down = P("expert", None, "dp"), P("expert", "dp", None)
    grid = Grid(mesh.shape["dp"], mesh.shape["expert"])
    return jax.shard_map(
        partial(body, grid),
        mesh=mesh,
        in_specs=(image, P(None, BOTH), row, row, rows, rows, row, row, rows, up, down, image),
        out_specs=(image, image, row, row, rows, rows, row, row, rows, up, down),
        check_vma=False,
    )
```

time: 619 us -> 469 us (0.76)
  matrix products: 185 us -> 28.1 us
  other arithmetic: 148 us -> 36 us
  Pallas kernels: 0 us -> 105 us
  starting transfers between devices: 62.2 us -> 105 us
  local copies, waits for them, and re-layouts: 106 us -> 77.7 us
    dot_general x27 -> x8, matrix products: 185 us -> 28.1 us  [the longest x2 19.9 us: dot(): lax.dot_general(a, b, (((ca,), (cb,)), ((), ())), preferred_element_type=...]
    pallas_call x0 -> x3, Pallas kernels: none -> 105 us  [the longest x1 46.3 us: backward(): call(partial(backward_kernel, tokens, slots), images, [image, own(keys, 3...]
    convert_element_type x12 -> x3, other arithmetic: 67.5 us -> 3.23 us  [the longest x1 3.13 us: experts(): active = active.astype(BF16)]
    reduce_sum x9 -> x1, other arithmetic: 54.7 us -> 6.04 us  [body(): total = jnp.sum(grad_triple.astype(F32), axis=0, keepdims=True)]
    ppermute x44, starting transfers between devices: 62.2 us -> 105 us  [send(): return lax.ppermute(a, BOTH, self.perm(axis, k))]
    optimization_barrier x2 -> x0, local copies, waits for them, and re-layouts: 22.7 us -> none  [the longest x1 16.4 us: round_down(): return lax.optimization_barrier(v.astype(jnp.bfloat16)).astype(jnp.float32)]
    convert_element_type x7 -> x3, local copies, waits for them, and re-layouts: 16.9 us -> 3.03 us  [the longest x2 2.43 us: body(): a.astype(BF16).reshape(per, grid.n, grid.m, step, features)]
    another operation x13 -> x15, local copies, waits for them, and re-layouts: 21 us -> 8.63 us  [the longest x1 3.87 us: body(): arrived = arrived.reshape(grid.n * grid.m, per, 2, step, features)]
  transfers between devices with their start and end apart: 44 -> 44, of which waited for: 27 -> 26; matrix products, arithmetic and copies ran while one was open for 10% -> 10% of each run, Pallas kernels for 0% -> 4%
where the time goes in v2:
time: 469 us; the launch traced here: 461 us
  waiting for transfers between devices  107 us (23%)
  starting transfers between devices  105 us (22%)
  Pallas kernels  105 us (22%)
  local copies, waits for them, and re-layouts  77.7 us (17%)
  other arithmetic  36 us (8%)
  matrix products  28.1 us (6%)
    ppermute x44, waiting for transfers between devices, send(): return lax.ppermute(a, BOTH, self.perm(axis, k))  107 us
    ppermute x44, starting transfers between devices, send(): return lax.ppermute(a, BOTH, self.perm(axis, k))  105 us
    pallas_call x1, Pallas kernels, backward(): call(partial(backward_kernel, tokens, slots), images, [image, own(keys, 3...  46.3 us
    pallas_call x1, Pallas kernels, forward(): call(partial(forward_kernel, tokens, slots), images, [image, image, fixed...  40.6 us
    unnamed x64, local copies, waits for them, and re-layouts  28.1 us
    dot_general x2, matrix products, dot(): lax.dot_general(a, b, (((ca,), (cb,)), ((), ())), preferred_element_type=...  19.9 us
    pallas_call x1, Pallas kernels, input_backward(): call(partial(input_kernel, tokens), images, [image_spec(tokens, features,...  18.5 us
  transfers between devices with their start and end apart: 44, of which 26 were waited for; matrix products, arithmetic and copies ran while one was open for 10% of the time, Pallas kernels for 4%

profile of v2, /device:TPU:0, one launch (start us, length us, event | category | flops | bytes accessed | tf_op | source)
XLA Modules:
  0.0 461.1 jit_solution(12166979022750406902)
XLA Ops:
  5.4 4.1 collective-permute-start.7
  26.5 6.8 %collective-permute-done.3 = bf16[4,24,1664]{2,1,0:T(8,128)(2,1)S(1)} collective-permute-done((bf16[4,24,1664]{2,1,0:T(8,128)(2,1)S(1)}, bf16[4,24,1664]{2,1,0:T(8,128)(2,1)S(1)}, u32[]{:S(2)}, u32[]{:S(2)}) %collective-permute-start.3) | collective-permute-done | bytes 319520 | tf_op jit(solution)/shard_map/ppermute | solution.py:42
  35.1 8.1 %collective-permute-done.10 = bf16[2,4,24,1536]{3,2,0,1:T(8,128)(2,1)S(1)} collective-permute-done((bf16[2,4,24,1536]{3,2,0,1:T(8,128)(2,1)S(1)}, bf16[2,4,24,1536]{3,2,0,1:T(8,128)(2,1)S(1)}, u32[]{:S(2)}, u32[]{:S(2)}) %collective-permute-start.10) | collective-permute-done | bytes 589856 | tf_op jit(solution)/shard_map/ppermute | solution.py:42
  47.0 4.4 copy.180.cot_ref
  62.8 40.6 %shard_map.203 = (bf16[12,208,768]{2,1,0:T(8,128)(2,1)}, bf16[12,256,2304]{2,1,0:T(8,128)(2,1)}, bf16[12,208,768]{2,1,0:T(8,128)(2,1)}, f32[12,208,768]{2,1,0:T(...) custom-call(s32[12]{0:T(128)} %reshape.137.live, ...), custom_call_target="tpu_custom_call" | custom-call | tf_op jit(solution)/shard_map/pallas_call | solution.py:345
  106.3 5.1 %collective-permute-done.12 = bf16[2,48,768]{2,1,0:T(8,128)(2,1)S(1)} collective-permute-done((bf16[2,48,768]{2,1,0:T(8,128)(2,1)S(1)}, bf16[2,48,768]{2,1,0:T(8,128)(2,1)S(1)}, u32[]{:S(2)}, u32[]{:S(2)}) %collective-permute-start.12) | collective-permute-done | bytes 147488 | tf_op jit(solution)/shard_map/ppermute | solution.py:42
  111.4 5.9 %collective-permute-start.13 = (bf16[2,48,768]{2,1,0:T(8,128)(2,1)S(1)}, bf16[2,48,768]{2,1,0:T(8,128)(2,1)S(1)}, u32[]{:S(2)}, u32[]{:S(2)}) collective-permute-start(bf16[2,48,768]{2,1,0:T(8,128)(2,1)S(1)} %fusion.47), channel_id=1, source_target_pairs={{0,1},{1,0},{2,3},{3,2},{4,5},{5,4},{6,7},{7,6},{8,9},{9,8},{10,11... | collective-permute-start | bytes 442376 | tf_op jit(solution)/shard_map/ppermute | solution.py:42
  118.5 11.4 %collective-permute-start.18 = (bf16[4,16,768]{2,1,0:T(8,128)(2,1)S(1)}, bf16[4,16,768]{2,1,0:T(8,128)(2,1)S(1)}, u32[]{:S(2)}, u32[]{:S(2)}) collective-permute-start(bf16[4,16,768]{2,1,0:T(8,128)(2,1)S(1)} %slice.139), channel_id=1, source_target_pairs={{0,4},{1,5},{2,6},{3,7},{4,0},{5,1},{6,2},{7,3},{8,12},{9,13},{10,... | collective-permute-start | bytes 294920 | tf_op jit(solution)/shard_map/ppermute | solution.py:42
  129.9 5.8 %collective-permute-start.15 = (bf16[4,32,768]{2,1,0:T(8,128)(2,1)S(1)}, bf16[4,32,768]{2,1,0:T(8,128)(2,1)S(1)}, u32[]{:S(2)}, u32[]{:S(2)}) collective-permute-start(bf16[4,32,768]{2,1,0:T(8,128)(2,1)S(1)} %slice.138), channel_id=1, source_target_pairs={{0,16},{1,17},{2,18},{3,19},{4,20},{5,21},{6,22},{7,23},{8,24},{9,... | collective-permute-start | bytes 589832 | tf_op jit(solution)/shard_map/ppermute | solution.py:42
  135.7 5.0 %collective-permute-start.16 = (bf16[4,32,768]{2,1,0:T(8,128)(2,1)S(1)}, bf16[4,32,768]{2,1,0:T(8,128)(2,1)S(1)}, u32[]{:S(2)}, u32[]{:S(2)}) collective-permute-start(bf16[4,32,768]{2,1,0:T(8,128)(2,1)S(1)} %slice.138), channel_id=1, source_target_pairs={{0,24},{1,25},{2,26},{3,27},{4,28},{5,29},{6,30},{7,31},{8,0},{9,1... | collective-permute-start | bytes 589832 | tf_op jit(solution)/shard_map/ppermute | solution.py:42
  141.2 4.8 %collective-permute-done.16 = bf16[4,32,768]{2,1,0:T(8,128)(2,1)S(1)} collective-permute-done((bf16[4,32,768]{2,1,0:T(8,128)(2,1)S(1)}, bf16[4,32,768]{2,1,0:T(8,128)(2,1)S(1)}, u32[]{:S(2)}, u32[]{:S(2)}) %collective-permute-start.16) | collective-permute-done | bytes 196640 | tf_op jit(solution)/shard_map/ppermute | solution.py:42
  146.0 8.0 %collective-permute-done.14 = bf16[4,32,768]{2,1,0:T(8,128)(2,1)S(1)} collective-permute-done((bf16[4,32,768]{2,1,0:T(8,128)(2,1)S(1)}, bf16[4,32,768]{2,1,0:T(8,128)(2,1)S(1)}, u32[]{:S(2)}, u32[]{:S(2)}) %collective-permute-start.14) | collective-permute-done | bytes 196640 | tf_op jit(solution)/shard_map/ppermute | solution.py:42
  161.1 8.5 %collective-permute-done.20 = bf16[2,4,16,768]{3,2,1,0:T(8,128)(2,1)S(1)} collective-permute-done((bf16[2,4,16,768]{3,2,1,0:T(8,128)(2,1)}, bf16[2,4,16,768]{3,2,1,0:T(8,128)(2,1)S(1)}, u32[]{:S(2)}, u32[]{:S(2)}) %collective-permute-start.20) | collective-permute-done | bytes 196640 | tf_op jit(solution)/shard_map/ppermute | solution.py:42
  177.9 3.9 reshape_reshape.13
  215.6 13.8 %collective-permute-done.27 = bf16[2,4,16,768]{3,1,2,0:T(4,128)(2,1)S(1)} collective-permute-done((bf16[2,4,16,768]{3,1,2,0:T(4,128)(2,1)S(1)}, bf16[2,4,16,768]{3,1,2,0:T(4,128)(2,1)S(1)}, u32[]{:S(2)}, u32[]{:S(2)}) %collective-permute-start.27) | collective-permute-done | bytes 196640 | tf_op jit(solution)/shard_map/ppermute | solution.py:42
  235.5 4.5 collective-permute-done.25
  240.0 9.6 %collective-permute-done.24 = bf16[4,32,768]{2,0,1:T(4,128)(2,1)S(1)} collective-permute-done((bf16[4,32,768]{2,0,1:T(4,128)(2,1)S(1)}, bf16[4,32,768]{2,0,1:T(4,128)(2,1)S(1)}, u32[]{:S(2)}, u32[]{:S(2)}) %collective-permute-start.24) | collective-permute-done | bytes 196640 | tf_op jit(solution)/shard_map/ppermute | solution.py:42
  256.8 5.8 %copy.198 = bf16[768,2304]{0,1:T(8,128)(2,1)} copy(bf16[768,2304]{1,0:T(8,128)(2,1)} %slice.134.wqkv_ref) | data formatting | bytes 7077888
  266.9 46.3 %shard_map.204 = (bf16[12,1,197,768]{3,2,1,0:T(8,128)(2,1)}, bf16[12,208,768]{2,1,0:T(8,128)(2,1)}, bf16[12,208,2304]{2,1,0:T(8,128)(2,1)}, f32[16,768]{1,0:T(8,128)}) custom-call(s32[12]{0:T(128)} %reshape.137.live, bf16[4,3,197,768]{3,2,1,0:T(8,128)(2,1)} %copy.180.cot_ref, bf16[12,256,2304]{2,1,0:T(8,128)(2,1)} %get-tuple-element.22.triple_ref, ...), custom_call_target="tpu_custom_call" | custom-call | tf_op jit(solution)/shard_map/pallas_call | solution.py:361
  314.0 6.0 %convert_reduce_fusion = f32[2304]{0:T(1024)S(1)} fusion(bf16[12,208,2304]{2,1,0:T(8,128)(2,1)} %get-tuple-element.28.grad_triple_ref), kind=kLoop, calls=%fused_computation | loop fusion | flops 11499264 | bytes 11510784 | tf_op jit(solution)/shard_map/reduce_sum | solution.py:444
  320.0 16.5 %fusion.2 = (bf16[768]{0:T(1024)(128)(2,1)S(1)}, bf16[768]{0:T(1024)(128)(2,1)S(1)}, bf16[768,2304]{0,1:T(8,128)(2,1)}) fusion(bf16[768,2304]{0,1:T(8,128)(2,1)S(1)} %copy-done.3, f32[2304]{0:T(1024)S(1)} %convert_reduce_fusion, f32[768]{0:T(1024)S(1)} %get-tuple-element.86, f32[768]{0:T(1024)S(1)} %get-tuple-element.85, ...), kind=kOutput, calls=%fused_computation.6 | convolution fusion | flops 8849127424 | bytes 22431744 | tf_op jit(solution)/shard_map/dot_general | solution.py:130
  340.1 5.1 %fusion.5 = bf16[768,3200]{0,1:T(8,128)(2,1)} fusion(bf16[768,12]{0,1:T(8,128)(2,1)S(1)} %concatenate.39, bf16[768,768]{0,1:T(8,128)(2,1)S(1)} %bitcast_convert_fusion, bf16[768,2304]{0,1:T(8,128)(2,1)} %get-tuple-element.89), kind=kLoop, calls=%fused_computation.12 | loop fusion | flops 19660800 | bytes 9652224 | tf_op jit(solution)/shard_map/concatenate | solution.py:450
  345.2 7.7 %copy.184 = bf16[768,3200]{1,0:T(8,128)(2,1)} copy(bf16[768,3200]{0,1:T(8,128)(2,1)} %fusion.5) | data formatting | bytes 9830400 | tf_op jit(solution)/shard_map/concatenate | solution.py:450
  370.8 18.5 %shard_map.205 = bf16[12,1,197,768]{3,2,1,0:T(8,128)(2,1)} custom-call(s32[12]{0:T(128)} %reshape.137.live, bf16[4,3,197,768]{3,2,1,0:T(8,128)(2,1)} %copy.157.x_ref, bf16[12,208,2304]{2,1,0:T(8,128)(2,1)} %get-tuple-element.28.grad_triple_ref, bf16[12,208,768]{2,1,0:T(8,128)(2,1)} %get-tuple-element.29.grad_branch_ref, bf16[2304,768]{1,0:T(8,128)(2,1)} %bitcast.298, ...), custom_call_target="tpu_custom_call" | custom-call | tf_op jit(solution)/shard_map/pallas_call | solution.py:375
  389.2 5.4 %copy.190 = bf16[4,3,197,768]{3,0,2,1:T(4,128)(2,1)} copy(bf16[4,3,197,768]{3,2,1,0:T(8,128)(2,1)} %bitcast.297) | data formatting | bytes 7262208
  396.2 4.2 collective-permute-start.33
  402.1 10.0 %collective-permute-start.39 = (bf16[4,2,24,1664]{3,2,1,0:T(8,128)(2,1)S(1)}, bf16[4,2,24,1664]{3,2,1,0:T(8,128)(2,1)S(1)}, u32[]{:S(2)}, u32[]{:S(2)}) collective-permute-start(bf16[4,2,24,1664]{3,2,1,0:T(8,128)(2,1)S(1)} %dynamic-slice_bitcast_fusion.2), channel_id=1, source_target_pairs={{0,2},{1,3},{2,0},{3,1},{4,6},{5,7},{6,4},{7,5},{8,10},{9,11},{10,... | collective-permute-start | bytes 1916936 | tf_op jit(solution)/shard_map/ppermute | solution.py:42
  413.4 11.3 %collective-permute-start.34 = (bf16[4,24,1536]{2,1,0:T(8,128)(2,1)S(1)}, bf16[4,24,1536]{2,1,0:T(8,128)(2,1)S(1)}, u32[]{:S(2)}, u32[]{:S(2)}) collective-permute-start(bf16[4,24,1536]{2,1,0:T(8,128)(2,1)S(1)} %dynamic-slice_bitcast_fusion.5), channel_id=1, source_target_pairs={{0,2},{1,3},{2,0},{3,1},{4,6},{5,7},{6,4},{7,5},{8,10},{9,11},{10,... | collective-permute-start | bytes 884744 | tf_op jit(solution)/shard_map/ppermute | solution.py:42
  427.5 6.0 %collective-permute-done.34 = bf16[4,24,1536]{2,1,0:T(8,128)(2,1)S(1)} collective-permute-done((bf16[4,24,1536]{2,1,0:T(8,128)(2,1)S(1)}, bf16[4,24,1536]{2,1,0:T(8,128)(2,1)S(1)}, u32[]{:S(2)}, u32[]{:S(2)}) %collective-permute-start.34) | collective-permute-done | bytes 294944 | tf_op jit(solution)/shard_map/ppermute | solution.py:42
  433.6 6.7 %collective-permute-start.36 = (bf16[24,1536]{1,0:T(8,128)(2,1)S(1)}, bf16[24,1536]{1,0:T(8,128)(2,1)S(1)}, u32[]{:S(2)}, u32[]{:S(2)}) collective-permute-start(bf16[24,1536]{1,0:T(8,128)(2,1)S(1)} %get-tuple-element.138), channel_id=1, source_target_pairs={{0,16},{1,17},{2,18},{3,19},{4,20},{5,21},{6,22},{7,23},{8,24},{9,... | collective-permute-start | bytes 221192 | tf_op jit(solution)/shard_map/ppermute | solution.py:42
  441.9 5.9 %collective-permute-done.36 = bf16[24,1536]{1,0:T(8,128)(2,1)S(1)} collective-permute-done((bf16[24,1536]{1,0:T(8,128)(2,1)S(1)}, bf16[24,1536]{1,0:T(8,128)(2,1)S(1)}, u32[]{:S(2)}, u32[]{:S(2)}) %collective-permute-start.36) | collective-permute-done | bytes 73760 | tf_op jit(solution)/shard_map/ppermute | solution.py:42
  456.0 4.0 collective-permute-done.42
  (255 shorter events, 149.5 us)
Async XLA Ops:
  5.4 11.0 %collective-permute-start.7 = (bf16[24,1536]{1,0:T(8,128)(2,1)S(1)}, bf16[24,1536]{1,0:T(8,128)(2,1)S(1)}, u32[]{:S(2)}, u32[]{:S(2)}) collective-permute-start(bf16[24,1536]{1,0:T(8,128)(2,1)S(1)} %fusion.55), channel_id=1, source_target_pairs={{0,16},{1,17},{2,18},{3,19},{4,20},{5,21},{6,22},{7,23},{8,24},{9,... | collective-permute-start | bytes 221192 | tf_op jit(solution)/shard_map/ppermute | solution.py:42
  12.4 8.8 %collective-permute-start.1 = (bf16[24,1664]{1,0:T(8,128)(2,1)S(1)}, bf16[24,1664]{1,0:T(8,128)(2,1)S(1)}, u32[]{:S(2)}, u32[]{:S(2)}) collective-permute-start(bf16[24,1664]{1,0:T(8,128)(2,1)S(1)} %slice.104), channel_id=1, source_target_pairs={{0,16},{1,17},{2,18},{3,19},{4,20},{5,21},{6,22},{7,23},{8,24},{9,... | collective-permute-start | bytes 239624 | tf_op jit(solution)/shard_map/ppermute | solution.py:42
  13.5 7.8 %collective-permute-start.2 = (bf16[24,1664]{1,0:T(8,128)(2,1)S(1)}, bf16[24,1664]{1,0:T(8,128)(2,1)S(1)}, u32[]{:S(2)}, u32[]{:S(2)}) collective-permute-start(bf16[24,1664]{1,0:T(8,128)(2,1)S(1)} %slice.104), channel_id=1, source_target_pairs={{0,24},{1,25},{2,26},{3,27},{4,28},{5,29},{6,30},{7,31},{8,0},{9,1... | collective-permute-start | bytes 239624 | tf_op jit(solution)/shard_map/ppermute | solution.py:42
  22.8 10.5 %collective-permute-start.3 = (bf16[4,24,1664]{2,1,0:T(8,128)(2,1)S(1)}, bf16[4,24,1664]{2,1,0:T(8,128)(2,1)S(1)}, u32[]{:S(2)}, u32[]{:S(2)}) collective-permute-start(bf16[4,24,1664]{2,1,0:T(8,128)(2,1)S(1)} %pad_maximum_fusion.8), channel_id=1, source_target_pairs={{0,4},{1,5},{2,6},{3,7},{4,0},{5,1},{6,2},{7,3},{8,12},{9,13},{10,... | collective-permute-start | bytes 958472 | tf_op jit(solution)/shard_map/ppermute | solution.py:42
  24.9 18.2 %collective-permute-start.10 = (bf16[2,4,24,1536]{3,2,0,1:T(8,128)(2,1)S(1)}, bf16[2,4,24,1536]{3,2,0,1:T(8,128)(2,1)S(1)}, u32[]{:S(2)}, u32[]{:S(2)}) collective-permute-start(bf16[2,4,24,1536]{3,2,0,1:T(8,128)(2,1)S(1)} %pad_maximum_fusion.7), channel_id=1, source_target_pairs={{0,4},{1,5},{2,6},{3,7},{4,0},{5,1},{6,2},{7,3},{8,12},{9,13},{10,... | collective-permute-start | bytes 1769480 | tf_op jit(solution)/shard_map/ppermute | solution.py:42
  33.5 10.9 %collective-permute-start.4 = (bf16[2,4,24,1664]{3,2,0,1:T(8,128)(2,1)S(1)}, bf16[2,4,24,1664]{3,2,0,1:T(8,128)(2,1)S(1)}, u32[]{:S(2)}, u32[]{:S(2)}) collective-permute-start(bf16[2,4,24,1664]{3,2,0,1:T(8,128)(2,1)S(1)} %pad_maximum_fusion.6), channel_id=1, source_target_pairs={{0,2},{1,3},{2,0},{3,1},{4,6},{5,7},{6,4},{7,5},{8,10},{9,11},{10,... | collective-permute-start | bytes 1916936 | tf_op jit(solution)/shard_map/ppermute | solution.py:42
  44.4 9.3 %collective-permute-start.11 = (bf16[2,2,4,24,1536]{4,3,1,0,2:T(8,128)(2,1)}, bf16[2,2,4,24,1536]{4,3,1,0,2:T(8,128)(2,1)}, u32[]{:S(2)}, u32[]{:S(2)}) collective-permute-start(bf16[2,2,4,24,1536]{4,3,1,0,2:T(8,128)(2,1)} %pad_maximum_fusion.3), channel_id=1, source_target_pairs={{0,1},{1,0},{2,3},{3,2},{4,5},{5,4},{6,7},{7,6},{8,9},{9,8},{10,11... | collective-permute-start | bytes 3538952 | tf_op jit(solution)/shard_map/ppermute | solution.py:42
  45.8 9.7 %collective-permute-start.5 = (bf16[2,2,4,24,1664]{4,3,0,1,2:T(8,128)(2,1)}, bf16[2,2,4,24,1664]{4,3,0,1,2:T(8,128)(2,1)}, u32[]{:S(2)}, u32[]{:S(2)}) collective-permute-start(bf16[2,2,4,24,1664]{4,3,0,1,2:T(8,128)(2,1)} %pad_maximum_fusion.2), channel_id=1, source_target_pairs={{0,1},{1,0},{2,3},{3,2},{4,5},{5,4},{6,7},{7,6},{8,9},{9,8},{10,11... | collective-permute-start | bytes 3833864 | tf_op jit(solution)/shard_map/ppermute | solution.py:42
  118.5 22.2 %collective-permute-start.18 = (bf16[4,16,768]{2,1,0:T(8,128)(2,1)S(1)}, bf16[4,16,768]{2,1,0:T(8,128)(2,1)S(1)}, u32[]{:S(2)}, u32[]{:S(2)}) collective-permute-start(bf16[4,16,768]{2,1,0:T(8,128)(2,1)S(1)} %slice.139), channel_id=1, source_target_pairs={{0,4},{1,5},{2,6},{3,7},{4,0},{5,1},{6,2},{7,3},{8,12},{9,13},{10,... | collective-permute-start | bytes 294920 | tf_op jit(solution)/shard_map/ppermute | solution.py:42
  129.9 11.3 %collective-permute-start.15 = (bf16[4,32,768]{2,1,0:T(8,128)(2,1)S(1)}, bf16[4,32,768]{2,1,0:T(8,128)(2,1)S(1)}, u32[]{:S(2)}, u32[]{:S(2)}) collective-permute-start(bf16[4,32,768]{2,1,0:T(8,128)(2,1)S(1)} %slice.138), channel_id=1, source_target_pairs={{0,16},{1,17},{2,18},{3,19},{4,20},{5,21},{6,22},{7,23},{8,24},{9,... | collective-permute-start | bytes 589832 | tf_op jit(solution)/shard_map/ppermute | solution.py:42
  135.7 10.3 %collective-permute-start.16 = (bf16[4,32,768]{2,1,0:T(8,128)(2,1)S(1)}, bf16[4,32,768]{2,1,0:T(8,128)(2,1)S(1)}, u32[]{:S(2)}, u32[]{:S(2)}) collective-permute-start(bf16[4,32,768]{2,1,0:T(8,128)(2,1)S(1)} %slice.138), channel_id=1, source_target_pairs={{0,24},{1,25},{2,26},{3,27},{4,28},{5,29},{6,30},{7,31},{8,0},{9,1... | collective-permute-start | bytes 589832 | tf_op jit(solution)/shard_map/ppermute | solution.py:42
  140.7 13.3 %collective-permute-start.14 = (bf16[4,32,768]{2,1,0:T(8,128)(2,1)S(1)}, bf16[4,32,768]{2,1,0:T(8,128)(2,1)S(1)}, u32[]{:S(2)}, u32[]{:S(2)}) collective-permute-start(bf16[4,32,768]{2,1,0:T(8,128)(2,1)S(1)} %slice.138), channel_id=1, source_target_pairs={{0,8},{1,9},{2,10},{3,11},{4,12},{5,13},{6,14},{7,15},{8,16},{9,17... | collective-permute-start | bytes 589832 | tf_op jit(solution)/shard_map/ppermute | solution.py:42
  154.2 19.4 %collective-permute-start.17 = (bf16[4,4,32,768]{3,2,1,0:T(8,128)(2,1)S(1)}, bf16[4,4,32,768]{3,2,1,0:T(8,128)(2,1)}, u32[]{:S(2)}, u32[]{:S(2)}) collective-permute-start(bf16[4,4,32,768]{3,2,1,0:T(8,128)(2,1)S(1)} %pad_maximum_fusion.4), channel_id=1, source_target_pairs={{0,4},{1,5},{2,6},{3,7},{4,0},{5,1},{6,2},{7,3},{8,12},{9,13},{10,... | collective-permute-start | bytes 2359304 | tf_op jit(solution)/shard_map/ppermute | solution.py:42
  155.4 14.3 %collective-permute-start.20 = (bf16[2,4,16,768]{3,2,1,0:T(8,128)(2,1)}, bf16[2,4,16,768]{3,2,1,0:T(8,128)(2,1)S(1)}, u32[]{:S(2)}, u32[]{:S(2)}) collective-permute-start(bf16[2,4,16,768]{3,2,1,0:T(8,128)(2,1)} %pad_maximum_fusion.11), channel_id=1, source_target_pairs={{0,16},{1,17},{2,18},{3,19},{4,20},{5,21},{6,22},{7,23},{8,24},{9,... | collective-permute-start | bytes 589832 | tf_op jit(solution)/shard_map/ppermute | solution.py:42
  158.9 14.6 %collective-permute-start.21 = (bf16[2,4,16,768]{3,2,1,0:T(8,128)(2,1)}, bf16[2,4,16,768]{3,2,1,0:T(8,128)(2,1)S(1)}, u32[]{:S(2)}, u32[]{:S(2)}) collective-permute-start(bf16[2,4,16,768]{3,2,1,0:T(8,128)(2,1)} %pad_maximum_fusion.11), channel_id=1, source_target_pairs={{0,24},{1,25},{2,26},{3,27},{4,28},{5,29},{6,30},{7,31},{8,0},{9,1... | collective-permute-start | bytes 589832 | tf_op jit(solution)/shard_map/ppermute | solution.py:42
  159.3 14.2 %collective-permute-start.19 = (bf16[2,4,16,768]{3,2,1,0:T(8,128)(2,1)}, bf16[2,4,16,768]{3,2,1,0:T(8,128)(2,1)S(1)}, u32[]{:S(2)}, u32[]{:S(2)}) collective-permute-start(bf16[2,4,16,768]{3,2,1,0:T(8,128)(2,1)} %pad_maximum_fusion.11), channel_id=1, source_target_pairs={{0,8},{1,9},{2,10},{3,11},{4,12},{5,13},{6,14},{7,15},{8,16},{9,17... | collective-permute-start | bytes 589832 | tf_op jit(solution)/shard_map/ppermute | solution.py:42
  206.4 25.0 %collective-permute-start.22 = (bf16[4,4,32,768]{3,1,2,0:T(4,128)(2,1)}, bf16[4,4,32,768]{3,1,2,0:T(4,128)(2,1)}, u32[]{:S(2)}, u32[]{:S(2)}) collective-permute-start(bf16[4,4,32,768]{3,1,2,0:T(4,128)(2,1)} %dynamic-slice_bitcast_fusion.1), channel_id=1, source_target_pairs={{0,4},{1,5},{2,6},{3,7},{4,0},{5,1},{6,2},{7,3},{8,12},{9,13},{10,... | collective-permute-start | bytes 2359304 | tf_op jit(solution)/shard_map/ppermute | solution.py:42
  207.3 8.3 %collective-permute-start.28 = (bf16[2,4,16,768]{3,1,2,0:T(4,128)(2,1)S(1)}, bf16[2,4,16,768]{3,1,2,0:T(4,128)(2,1)S(1)}, u32[]{:S(2)}, u32[]{:S(2)}) collective-permute-start(bf16[2,4,16,768]{3,1,2,0:T(4,128)(2,1)S(1)} %get-tuple-element.109), channel_id=1, source_target_pairs={{0,24},{1,25},{2,26},{3,27},{4,28},{5,29},{6,30},{7,31},{8,0},{9,1... | collective-permute-start | bytes 589832 | tf_op jit(solution)/shard_map/ppermute | solution.py:42
  209.0 20.4 %collective-permute-start.27 = (bf16[2,4,16,768]{3,1,2,0:T(4,128)(2,1)S(1)}, bf16[2,4,16,768]{3,1,2,0:T(4,128)(2,1)S(1)}, u32[]{:S(2)}, u32[]{:S(2)}) collective-permute-start(bf16[2,4,16,768]{3,1,2,0:T(4,128)(2,1)S(1)} %get-tuple-element.110), channel_id=1, source_target_pairs={{0,16},{1,17},{2,18},{3,19},{4,20},{5,21},{6,22},{7,23},{8,24},{9,... | collective-permute-start | bytes 589832 | tf_op jit(solution)/shard_map/ppermute | solution.py:42
  212.5 17.0 %collective-permute-start.26 = (bf16[2,4,16,768]{3,1,2,0:T(4,128)(2,1)S(1)}, bf16[2,4,16,768]{3,1,2,0:T(4,128)(2,1)S(1)}, u32[]{:S(2)}, u32[]{:S(2)}) collective-permute-start(bf16[2,4,16,768]{3,1,2,0:T(4,128)(2,1)S(1)} %get-tuple-element.108), channel_id=1, source_target_pairs={{0,8},{1,9},{2,10},{3,11},{4,12},{5,13},{6,14},{7,15},{8,16},{9,17... | collective-permute-start | bytes 589832 | tf_op jit(solution)/shard_map/ppermute | solution.py:42
  233.4 16.2 %collective-permute-start.24 = (bf16[4,32,768]{2,0,1:T(4,128)(2,1)S(1)}, bf16[4,32,768]{2,0,1:T(4,128)(2,1)S(1)}, u32[]{:S(2)}, u32[]{:S(2)}) collective-permute-start(bf16[4,32,768]{2,0,1:T(4,128)(2,1)S(1)} %get-tuple-element.113), channel_id=1, source_target_pairs={{0,16},{1,17},{2,18},{3,19},{4,20},{5,21},{6,22},{7,23},{8,24},{9,... | collective-permute-start | bytes 589832 | tf_op jit(solution)/shard_map/ppermute | solution.py:42
  233.5 16.1 %collective-permute-start.23 = (bf16[4,32,768]{2,0,1:T(4,128)(2,1)S(1)}, bf16[4,32,768]{2,0,1:T(4,128)(2,1)S(1)}, u32[]{:S(2)}, u32[]{:S(2)}) collective-permute-start(bf16[4,32,768]{2,0,1:T(4,128)(2,1)S(1)} %get-tuple-element.111), channel_id=1, source_target_pairs={{0,8},{1,9},{2,10},{3,11},{4,12},{5,13},{6,14},{7,15},{8,16},{9,17... | collective-permute-start | bytes 589832 | tf_op jit(solution)/shard_map/ppermute | solution.py:42
  255.2 8.1 %collective-permute-start.31 = (bf16[2,48,768]{2,1,0:T(8,128)(2,1)S(1)}, bf16[2,48,768]{2,1,0:T(8,128)(2,1)S(1)}, u32[]{:S(2)}, u32[]{:S(2)}) collective-permute-start(bf16[2,48,768]{2,1,0:T(8,128)(2,1)S(1)} %fusion.43), channel_id=1, source_target_pairs={{0,1},{1,0},{2,3},{3,2},{4,5},{5,4},{6,7},{7,6},{8,9},{9,8},{10,11... | collective-permute-start | bytes 442376 | tf_op jit(solution)/shard_map/ppermute | solution.py:42
  357.1 37.5 %collective-permute-start.32 = (bf16[4,2,2,24,1536]{4,3,0,2,1:T(8,128)(2,1)}, bf16[4,2,2,24,1536]{4,3,0,2,1:T(8,128)(2,1)}, u32[]{:S(2)}, u32[]{:S(2)}) collective-permute-start(bf16[4,2,2,24,1536]{4,3,0,2,1:T(8,128)(2,1)} %bitcast.289), channel_id=1, source_target_pairs={{0,1},{1,0},{2,3},{3,2},{4,5},{5,4},{6,7},{7,6},{8,9},{9,8},{10,11... | collective-permute-start | bytes 3538952 | tf_op jit(solution)/shard_map/ppermute | solution.py:42
  361.6 38.8 %collective-permute-start.38 = (bf16[4,2,2,24,1664]{4,3,2,1,0:T(8,128)(2,1)}, bf16[4,2,2,24,1664]{4,3,2,1,0:T(8,128)(2,1)}, u32[]{:S(2)}, u32[]{:S(2)}) collective-permute-start(bf16[4,2,2,24,1664]{4,3,2,1,0:T(8,128)(2,1)} %dynamic-slice_bitcast_fusion), channel_id=1, source_target_pairs={{0,1},{1,0},{2,3},{3,2},{4,5},{5,4},{6,7},{7,6},{8,9},{9,8},{10,11... | collective-permute-start | bytes 3833864 | tf_op jit(solution)/shard_map/ppermute | solution.py:42
  396.2 17.0 %collective-permute-start.33 = (bf16[4,2,24,1536]{3,2,0,1:T(8,128)(2,1)S(1)}, bf16[4,2,24,1536]{3,2,0,1:T(8,128)(2,1)S(1)}, u32[]{:S(2)}, u32[]{:S(2)}) collective-permute-start(bf16[4,2,24,1536]{3,2,0,1:T(8,128)(2,1)S(1)} %dynamic-slice_bitcast_fusion.3), channel_id=1, source_target_pairs={{0,4},{1,5},{2,6},{3,7},{4,0},{5,1},{6,2},{7,3},{8,12},{9,13},{10,... | collective-permute-start | bytes 1769480 | tf_op jit(solution)/shard_map/ppermute | solution.py:42
  402.1 25.2 %collective-permute-start.39 = (bf16[4,2,24,1664]{3,2,1,0:T(8,128)(2,1)S(1)}, bf16[4,2,24,1664]{3,2,1,0:T(8,128)(2,1)S(1)}, u32[]{:S(2)}, u32[]{:S(2)}) collective-permute-start(bf16[4,2,24,1664]{3,2,1,0:T(8,128)(2,1)S(1)} %dynamic-slice_bitcast_fusion.2), channel_id=1, source_target_pairs={{0,2},{1,3},{2,0},{3,1},{4,6},{5,7},{6,4},{7,5},{8,10},{9,11},{10,... | collective-permute-start | bytes 1916936 | tf_op jit(solution)/shard_map/ppermute | solution.py:42
  413.4 20.0 %collective-permute-start.34 = (bf16[4,24,1536]{2,1,0:T(8,128)(2,1)S(1)}, bf16[4,24,1536]{2,1,0:T(8,128)(2,1)S(1)}, u32[]{:S(2)}, u32[]{:S(2)}) collective-permute-start(bf16[4,24,1536]{2,1,0:T(8,128)(2,1)S(1)} %dynamic-slice_bitcast_fusion.5), channel_id=1, source_target_pairs={{0,2},{1,3},{2,0},{3,1},{4,6},{5,7},{6,4},{7,5},{8,10},{9,11},{10,... | collective-permute-start | bytes 884744 | tf_op jit(solution)/shard_map/ppermute | solution.py:42
  433.6 8.3 %collective-permute-start.37 = (bf16[24,1536]{1,0:T(8,128)(2,1)S(1)}, bf16[24,1536]{1,0:T(8,128)(2,1)S(1)}, u32[]{:S(2)}, u32[]{:S(2)}) collective-permute-start(bf16[24,1536]{1,0:T(8,128)(2,1)S(1)} %get-tuple-element.137), channel_id=1, source_target_pairs={{0,24},{1,25},{2,26},{3,27},{4,28},{5,29},{6,30},{7,31},{8,0},{9,1... | collective-permute-start | bytes 221192 | tf_op jit(solution)/shard_map/ppermute | solution.py:42
  433.6 14.1 %collective-permute-start.36 = (bf16[24,1536]{1,0:T(8,128)(2,1)S(1)}, bf16[24,1536]{1,0:T(8,128)(2,1)S(1)}, u32[]{:S(2)}, u32[]{:S(2)}) collective-permute-start(bf16[24,1536]{1,0:T(8,128)(2,1)S(1)} %get-tuple-element.138), channel_id=1, source_target_pairs={{0,16},{1,17},{2,18},{3,19},{4,20},{5,21},{6,22},{7,23},{8,24},{9,... | collective-permute-start | bytes 221192 | tf_op jit(solution)/shard_map/ppermute | solution.py:42
  440.3 7.5 %collective-permute-start.35 = (bf16[24,1536]{1,0:T(8,128)(2,1)S(1)}, bf16[24,1536]{1,0:T(8,128)(2,1)S(1)}, u32[]{:S(2)}, u32[]{:S(2)}) collective-permute-start(bf16[24,1536]{1,0:T(8,128)(2,1)S(1)} %get-tuple-element.136), channel_id=1, source_target_pairs={{0,8},{1,9},{2,10},{3,11},{4,12},{5,13},{6,14},{7,15},{8,16},{9,17... | collective-permute-start | bytes 221192 | tf_op jit(solution)/shard_map/ppermute | solution.py:42
  440.3 9.5 %collective-permute-start.40 = (bf16[4,24,1664]{2,1,0:T(8,128)(2,1)S(1)}, bf16[4,24,1664]{2,1,0:T(8,128)(2,1)S(1)}, u32[]{:S(2)}, u32[]{:S(2)}) collective-permute-start(bf16[4,24,1664]{2,1,0:T(8,128)(2,1)S(1)} %dynamic-slice_bitcast_fusion.4), channel_id=1, source_target_pairs={{0,4},{1,5},{2,6},{3,7},{4,0},{5,1},{6,2},{7,3},{8,12},{9,13},{10,... | collective-permute-start | bytes 958472 | tf_op jit(solution)/shard_map/ppermute | solution.py:42
  (38 other events, 462.3 us)
